TPU v7x, 32 devices: a whole 2x2x4 slice. The times are simulated.
32 devices in a mesh: section: 2 (over y), dp: 16 (over z, x, core).
Axes of the slice: x: 2, y: 2, z: 4, core: 2. Of those that a mesh axis runs over, the one named last changes fastest.
Arguments:
- layer_input: bfloat16 [2, 4096, 4, 128], P('section', 'dp'), may hold values from 0 to 1
- gate_weight: bfloat16 [2, 4096, 16384], P('section', None, 'dp'), may hold values from -0.09375 to 0.09375
- up_weight: bfloat16 [2, 4096, 16384], P('section', None, 'dp'), may hold values from -0.09375 to 0.09375
- down_weight: bfloat16 [2, 16384, 4096], P('section', 'dp'), may hold values from -0.046875 to 0.046875
- hidden_threshold: int32 [2, 16384], P('section', 'dp'), may hold values from 1 to 5
- hidden_width: int32 [2, 16384], P('section', 'dp'), may hold values from 1 to 5
- out_threshold: int32 [2, 4096], P('section', 'dp'), may hold values from 1 to 5
- out_width: int32 [2, 4096], P('section', 'dp'), may hold values from 1 to 5
- out_cotangent: bfloat16 [2, 4096, 4, 128], P('section', 'dp'), may hold values from -6 to 6
Outputs:
- incoming_spikes: bfloat16 [2, 4096, 4, 128], P('section', 'dp')
- returned_grads: bfloat16 [2, 4096, 4, 128], P('section', 'dp')
All inputs are finite; a program needn't handle non-finite values.
Results may differ from a plain program's by a relative error of at most 0.013.
Values may be sent and summed in bfloat16 or wider, within the bound.
No kernel may reach another device: no remote copies, remote signals or barrier semaphores. Data moves between devices by JAX's collectives and lax.ppermute only.
A program may use at most 128 MiB of HBM per device.

v0:
```python
import jax
import jax.numpy as jnp
from jax import lax
from jax.sharding import PartitionSpec as P

T_STEPS = 4


decay_rate = 0.9
level_unit = 0.125


def with_halo(block, sides, width):
    for axis, dim in sides:
        count = lax.axis_size(axis)
        forward = [(i, i + 1) for i in range(count - 1)]
        backward = [(target, source) for source, target in forward]
        low = lax.ppermute(
            lax.slice_in_dim(block, block.shape[dim] - width, None, axis=dim), axis, forward
        )
        high = lax.ppermute(lax.slice_in_dim(block, 0, width, axis=dim), axis, backward)
        block = jnp.concatenate([low, block, high], axis=dim)
    return block


def soft_spikes(currents, threshold_level, width_level):
    threshold = level_unit * threshold_level.astype(currents[0].dtype)
    width = level_unit * width_level.astype(currents[0].dtype)
    potential = jnp.zeros_like(currents[0])
    spikes = jnp.zeros_like(currents[0])
    emitted = []
    for current in currents:
        potential = decay_rate * (potential - threshold * spikes) + current
        spikes = jax.nn.sigmoid((potential - threshold) / width)
        emitted.append(spikes)
    return emitted


def split_steps(matrix, count, axis):
    return [lax.slice_in_dim(matrix, k * count, (k + 1) * count, axis=axis) for k in range(T_STEPS)]


def contract(left, right, left_dim, right_dim):
    return lax.dot_general(
        left, right, (((left_dim,), (right_dim,)), ((), ())), preferred_element_type=jnp.float32
    )


def per_device(
    layer_input,
    gate_weight,
    up_weight,
    down_weight,
    hidden_threshold,
    hidden_width,
    out_threshold,
    out_width,
    out_cotangent,
):
    local_rows = layer_input.shape[1]
    steps_count = layer_input.shape[2]
    tokens = layer_input.shape[3]
    rows = steps_count * tokens
    gate_w = gate_weight[0]
    up_w = up_weight[0]
    down_w = down_weight[0]

    def hidden_fn(gate_in, up_in):
        return soft_spikes(
            split_steps(jax.nn.silu(gate_in) * up_in, tokens, 0),
            hidden_threshold[0],
            hidden_width[0],
        )

    piece = lax.all_gather(layer_input, "dp", axis=1, tiled=True)
    count = piece.shape[1]
    flat = piece.reshape(count, rows)
    gate_part = gate_w
    up_part = up_w
    gate = contract(flat, gate_part, 0, 0)
    upward = contract(flat, up_part, 0, 0)
    hidden_list, hidden_back = jax.vjp(hidden_fn, gate, upward)
    spikes = jnp.concatenate(hidden_list, 0).astype(jnp.bfloat16)
    part = down_w
    projected = lax.psum_scatter(
        contract(part, spikes, 0, 1), "dp", scatter_dimension=0, tiled=True
    )
    current = projected + layer_input[0].reshape(local_rows, rows).astype(jnp.float32)
    level_own = out_threshold[0][:, None]
    spread_own = out_width[0][:, None]

    def out_fn(total):
        return soft_spikes(split_steps(total, tokens, 1), level_own, spread_own)

    out_list, out_back = jax.vjp(out_fn, current)
    emitted = jnp.concatenate(out_list, 1).astype(jnp.bfloat16)
    cotangent = out_cotangent[0].reshape(local_rows, rows).astype(jnp.float32)
    current_grad = out_back(split_steps(cotangent, tokens, 1))[0]
    grad_block = current_grad.astype(jnp.bfloat16).reshape(1, local_rows, steps_count, tokens)
    piece = lax.all_gather(grad_block, "dp", axis=1, tiled=True)
    count = piece.shape[1]
    flat = piece.reshape(count, rows)
    part = down_w
    spike_grad = contract(flat, part, 0, 1)
    emitted_block = emitted.reshape(1, local_rows, steps_count, tokens)
    gate_grad, up_grad = hidden_back(split_steps(spike_grad, tokens, 0))
    gate_grad = gate_grad.astype(jnp.bfloat16)
    up_grad = up_grad.astype(jnp.bfloat16)
    gate_part = gate_w
    up_part = up_w
    summed = lax.psum_scatter(
        (contract(gate_part, gate_grad, 1, 1) + contract(up_part, up_grad, 1, 1)).astype(
            jnp.bfloat16
        ),
        "dp",
        scatter_dimension=0,
        tiled=True,
    ).astype(jnp.float32)
    input_grad = (
        (summed + current_grad).astype(jnp.bfloat16).reshape(1, local_rows, steps_count, tokens)
    )
    stacked = jnp.concatenate([input_grad, emitted_block], 0)
    extended = with_halo(stacked, (("section", 0),), 1)
    incoming = extended[0:1]
    returned = extended[3:4]
    return (incoming, returned)


def solution(mesh):
    placed = (
        P("section", "dp", None, None),
        P("section", None, "dp"),
        P("section", None, "dp"),
        P("section", "dp", None),
        P("section", "dp"),
        P("section", "dp"),
        P("section", "dp"),
        P("section", "dp"),
        P("section", "dp", None, None),
    )
    return jax.shard_map(
        per_device,
        mesh=mesh,
        in_specs=placed,
        out_specs=(P("section", "dp", None, None), P("section", "dp", None, None)),
        check_vma=False,
    )
```

profile of v0, /device:TPU:0, one launch (start us, length us, event | category | flops | bytes accessed | tf_op | source)
XLA Modules:
  0.0 370.9 jit_solution(11366145145992832953)
XLA Ops:
  7.2 0.7 all-gather.3.cloned.1.call-update
  7.9 0.7 convert_multiply_fusion.1
  8.6 0.7 convert_multiply_fusion
  9.3 54.1 %all-gather.3.cloned.1.call-done = bf16[1,4096,4,128]{3,2,0,1:T(4,128)(2,1)} async-done(((bf16[1,256,4,128]{3,2,0,1:T(4,128)(2,1)}), bf16[1,4096,4,128]{3,2,0,1:T(4,128)(2,1)}) %all-gather.3.cloned.1.call-update) | async-done | bytes 4194320 | tf_op jit(solution)/shard_map/all_gather | solution.py:75
  63.5 8.3 %fusion.10 = f32[512,1024]{1,0:T(8,128)S(1)} fusion(bf16[1,4096,1024]{2,1,0:T(8,128)(2,1)} %param.10, bf16[512,8,4,128]{3,2,1,0:T(4,128)(2,1)} %bitcast.72), kind=kOutput, calls=%fused_computation.10 | convolution fusion | flops 4294967296 | bytes 14680064 | tf_op jit(solution)/shard_map/dot_general | solution.py:44
  71.8 6.0 %fusion.55 = (f32[512,1024]{1,0:T(8,128)S(1)}, f32[512,1024]{1,0:T(8,128)}) fusion(f32[512,1024]{1,0:T(8,128)S(1)} %fusion.10, bf16[1,4096,1024]{2,1,0:T(8,128)(2,1)S(1)} %copy-done.15, bf16[512,8,4,128]{3,2,1,0:T(4,128)(2,1)S(1)} %bitcast.73), kind=kOutput, calls=%fused_computation.69 | convolution fusion | flops 4297588736 | bytes 18874368 | tf_op jit(solution)/shard_map/dot_general | solution.py:44
  78.5 1.2 fusion.91
  79.7 6.8 %fusion.12 = f32[4096,512]{0,1:T(8,128)} fusion(bf16[1,1024,4096]{2,1,0:T(8,128)(2,1)S(1)} %bitcast.71, bf16[128,1024]{1,0:T(8,128)(2,1)S(1)} %get-tuple-element.17, bf16[128,1024]{1,0:T(8,128)(2,1)S(1)} %get-tuple-element.15, bf16[128,1024]{1,0:T(8,128)(2,1)S(1)} %get-tuple-element.13, bf16[128,1024]{1,0:T(8,128)(2,1)S(1)} %get-tuple-element.19), kind=kOutput, calls=%fused_computation.13 | convolution fusion | flops 4299161600 | bytes 17825792 | tf_op jit(solution)/shard_map/dot_general | solution.py:44
  86.6 0.9 copy-done.3
  87.5 1.0 copy.16
  88.5 2.0 copy.18
  90.4 0.6 convert_multiply_fusion.2
  91.0 0.6 subtract_multiply_fusion.10
  91.6 98.5 %reduce-scatter.3.cloned.1.call-done = f32[256,512]{0,1:T(8,128)} async-done(((f32[4096,512]{0,1:T(8,128)}), f32[256,512]{0,1:T(8,128)}) %reduce-scatter.3.cloned.1.call-update) | async-done | bytes 524304 | tf_op jit(solution)/shard_map/reduce_scatter | solution.py:85
  190.1 1.3 bitcast_add_fusion
  191.3 2.0 fusion.67
  193.4 0.6 copy-done.1
  194.0 0.7 fusion.56
  195.0 52.9 %all-gather.5.cloned.1.call-done = bf16[1,4096,4,128]{1,3,2,0:T(8,128)(2,1)} async-done(((bf16[1,256,4,128]{1,3,2,0:T(8,128)(2,1)}), bf16[1,4096,4,128]{1,3,2,0:T(8,128)(2,1)}) %all-gather.5.cloned.1.call-update) | async-done | bytes 4194320 | tf_op jit(solution)/shard_map/all_gather | solution.py:100
  247.9 8.3 %fusion = f32[512,1024]{1,0:T(8,128)S(1)} fusion(bf16[4096,512]{0,1:T(8,128)(2,1)} %bitcast.74, bf16[1,1024,4096]{2,1,0:T(8,128)(2,1)} %param.12), kind=kOutput, calls=%fused_computation | convolution fusion | flops 4294967296 | bytes 14680064 | tf_op jit(solution)/shard_map/dot_general | solution.py:44
  256.2 0.8 fusion.47
  257.0 0.8 copy-done.18
  257.8 10.8 %fusion.4 = f32[512,4096]{1,0:T(8,128)} fusion(bf16[1,4096,1024]{2,1,0:T(8,128)(2,1)} %param.11, f32[128,1024]{1,0:T(8,128)S(1)} %get-tuple-element.2, f32[128,1024]{1,0:T(8,128)S(1)} %get-tuple-element.3, f32[128,1024]{1,0:T(8,128)S(1)} %get-tuple-element.4, f32[128,1024]{1,0:T(8,128)S(1)} %get-tuple-element.5, f32[512,1024]{1,0:T(8,128)S(1)} %copy-done.18), kind=kOutput, calls=%fused_computation.4 | convolution fusion | flops 4299685888 | bytes 20971520 | tf_op jit(solution)/shard_map/dot_general | solution.py:44
  268.6 13.9 %fusion.17 = bf16[4096,512]{0,1:T(8,128)(2,1)} fusion(f32[512,4096]{1,0:T(8,128)} %fusion.4, bf16[1,4096,1024]{2,1,0:T(8,128)(2,1)} %param.10, f32[512,1024]{1,0:T(8,128)S(1)} %copy-done.19, f32[512,1024]{1,0:T(8,128)} %get-tuple-element.24, f32[128,1024]{1,0:T(8,128)} %copy-done.5, f32[128,1024]{1,0:T(8,128)} %copy-done.6, f32[128,1024]{1,0:T(8,128)} %copy-done.7, ...), kind=kOutput, calls=%fused_computation.14 | convolution fusion | flops 4306501632 | bytes 27262976 | tf_op jit(solution)/shard_map/dot_general | solution.py:44
  282.6 0.8 copy-done.4
  283.7 3.4 collective-permute-start
  287.1 66.4 %reduce-scatter.5.cloned.1.call-done = bf16[256,512]{0,1:T(8,128)(2,1)} async-done(((bf16[4096,512]{0,1:T(8,128)(2,1)}), bf16[256,512]{0,1:T(8,128)(2,1)}) %reduce-scatter.5.cloned.1.call-update) | async-done | bytes 262160 | tf_op jit(solution)/shard_map/reduce_scatter | solution.py:111
  353.5 1.0 add_convert_fusion.1
  354.7 1.3 collective-permute-start.1
  356.0 7.0 %collective-permute-done.1 = bf16[1,256,4,128]{3,2,1,0:T(4,128)(2,1)S(1)} collective-permute-done((bf16[1,256,4,128]{3,2,1,0:T(4,128)(2,1)S(1)}, bf16[1,256,4,128]{3,2,1,0:T(4,128)(2,1)S(1)}, u32[]{:S(2)}, u32[]{:S(2)}) %collective-permute-start.1) | collective-permute-done | bytes 262176 | tf_op jit(solution)/shard_map/ppermute | solution.py:21
  363.0 0.7 copy.33
  363.7 0.7 copy.34
  (56 shorter events, 1.6 us)
Async XLA Ops:
  7.2 56.3 %all-gather.3.cloned.1.call-start = ((), (), s32[]{:S(2)}) async-start(), calls=%async_computation.2 | async-start | bytes 4456448 | tf_op jit(solution)/shard_map/all_gather | solution.py:75
  7.9 182.2 %reduce-scatter.3.cloned.1.call-start = ((), (), s32[]{:S(2)}) async-start(), calls=%async_computation.3 | async-start | bytes 8912896 | tf_op jit(solution)/shard_map/reduce_scatter | solution.py:85
  63.4 8.4 %copy-start.15 = (bf16[1,4096,1024]{2,1,0:T(8,128)(2,1)S(1)}, bf16[1,4096,1024]{2,1,0:T(8,128)(2,1)}, u32[]{:S(2)}) copy-start(bf16[1,4096,1024]{2,1,0:T(8,128)(2,1)} %param.11) | copy-start | bytes 25165828
  63.5 8.4 %copy-start.16 = (bf16[1,4096,4,128]{3,2,0,1:T(4,128)(2,1)S(1)}, bf16[1,4096,4,128]{3,2,0,1:T(4,128)(2,1)}, u32[]{:S(2)}) copy-start(bf16[1,4096,4,128]{3,2,0,1:T(4,128)(2,1)} %all-gather.3.cloned.1.call-done) | copy-start | bytes 12582916
  63.5 16.3 %slice-start = ((s8[8388608]{0:T(1024)(128)(4,1)}), s8[4194304]{0:T(1024)(128)(4,1)S(1)}, s32[]{:S(2)}) async-start(s8[8388608]{0:T(1024)(128)(4,1)} %bitcast.70), calls=%async_computation.6 | async-start | bytes 8388608
  71.8 6.0 %copy-start.17 = (f32[512,1024]{1,0:T(8,128)}, f32[512,1024]{1,0:T(8,128)S(1)}, u32[]{:S(2)}) copy-start(f32[512,1024]{1,0:T(8,128)S(1)} %fusion.10) | copy-start | bytes 6291460
  71.8 7.9 %slice-start.1 = ((s8[8388608]{0:T(1024)(128)(4,1)}), s8[4194304]{0:T(1024)(128)(4,1)S(1)}, s32[]{:S(2)}) async-start(s8[8388608]{0:T(1024)(128)(4,1)} %bitcast.70), calls=%async_computation.7 | async-start | bytes 8388608
  86.5 0.9 copy-start.3
  86.5 3.9 %copy-start.14 = (s32[1,256]{1,0:T(1,128)S(1)}, s32[1,256]{1,0:T(1,128)}, u32[]{:S(2)}) copy-start(s32[1,256]{1,0:T(1,128)} %param.16) | copy-start | bytes 3076
  86.5 4.5 %copy-start.13 = (s32[1,256]{1,0:T(1,128)S(1)}, s32[1,256]{1,0:T(1,128)}, u32[]{:S(2)}) copy-start(s32[1,256]{1,0:T(1,128)} %param.15) | copy-start | bytes 3076
  86.5 161.4 %all-gather.5.cloned.1.call-start = ((), (), s32[]{:S(2)}) async-start(), calls=%async_computation.4 | async-start | bytes 4456448 | tf_op jit(solution)/shard_map/all_gather | solution.py:100
  193.4 0.6 copy-start.1
  194.8 158.7 %reduce-scatter.5.cloned.1.call-start = ((), (), s32[]{:S(2)}) async-start(), calls=%async_computation.5 | async-start | bytes 4456448 | tf_op jit(solution)/shard_map/reduce_scatter | solution.py:111
  247.9 8.3 %copy-start = (f32[128,1024]{1,0:T(8,128)S(1)}, f32[128,1024]{1,0:T(8,128)}, u32[]{:S(2)}) copy-start(f32[128,1024]{1,0:T(8,128)} %get-tuple-element.18) | copy-start | bytes 1572868
  256.2 1.6 copy-start.18
  257.0 11.6 %copy-start.5 = (f32[128,1024]{1,0:T(8,128)}, f32[128,1024]{1,0:T(8,128)S(1)}, u32[]{:S(2)}) copy-start(f32[128,1024]{1,0:T(8,128)S(1)} %get-tuple-element.2) | copy-start | bytes 1572868
  257.0 11.6 %copy-start.6 = (f32[128,1024]{1,0:T(8,128)}, f32[128,1024]{1,0:T(8,128)S(1)}, u32[]{:S(2)}) copy-start(f32[128,1024]{1,0:T(8,128)S(1)} %get-tuple-element.3) | copy-start | bytes 1572868
  257.0 11.6 %copy-start.7 = (f32[128,1024]{1,0:T(8,128)}, f32[128,1024]{1,0:T(8,128)S(1)}, u32[]{:S(2)}) copy-start(f32[128,1024]{1,0:T(8,128)S(1)} %get-tuple-element.4) | copy-start | bytes 1572868
  257.0 11.6 %copy-start.8 = (f32[128,1024]{1,0:T(8,128)}, f32[128,1024]{1,0:T(8,128)S(1)}, u32[]{:S(2)}) copy-start(f32[128,1024]{1,0:T(8,128)S(1)} %get-tuple-element.5) | copy-start | bytes 1572868
  257.8 10.8 %copy-start.19 = (f32[512,1024]{1,0:T(8,128)S(1)}, f32[512,1024]{1,0:T(8,128)}, u32[]{:S(2)}) copy-start(f32[512,1024]{1,0:T(8,128)} %copy-done.17) | copy-start | bytes 6291460
  282.5 0.9 copy-start.4
  282.5 0.9 copy-start.12
  282.5 1.0 copy-start.9
  282.5 1.0 copy-start.10
  282.5 1.0 copy-start.11
  282.5 71.0 %copy-start.2 = (f32[256,128]{0,1:T(8,128)S(1)}, f32[256,128]{0,1:T(8,128)}, u32[]{:S(2)}) copy-start(f32[256,128]{0,1:T(8,128)} %copy-done.1) | copy-start | bytes 393220
  283.7 72.3 %collective-permute-start = (bf16[1,256,4,128]{3,2,1,0:T(4,128)(2,1)S(1)}, bf16[1,256,4,128]{3,2,1,0:T(4,128)(2,1)S(1)}, u32[]{:S(2)}, u32[]{:S(2)}) collective-permute-start(bf16[1,256,4,128]{3,2,1,0:T(4,128)(2,1)S(1)} %copy.17), channel_id=1, source_target_pairs={{0,16},{1,17},{2,18},{3,19},{4,20},{5,21},{6,22},{7,23},{8,24},{9,... | collective-permute-start | bytes 786440 | tf_op jit(solution)/shard_map/ppermute | solution.py:18
  354.7 8.3 %collective-permute-start.1 = (bf16[1,256,4,128]{3,2,1,0:T(4,128)(2,1)S(1)}, bf16[1,256,4,128]{3,2,1,0:T(4,128)(2,1)S(1)}, u32[]{:S(2)}, u32[]{:S(2)}) collective-permute-start(bf16[1,256,4,128]{3,2,1,0:T(4,128)(2,1)S(1)} %copy.19), channel_id=1, source_target_pairs={{16,0},{17,1},{18,2},{19,3},{20,4},{21,5},{22,6},{23,7},{24,8},{25... | collective-permute-start | bytes 786440 | tf_op jit(solution)/shard_map/ppermute | solution.py:21
Sparse Core Ops, SparseCore 0:
  10.2 53.2 all-gather.2
  86.7 103.3 reduce-scatter.2
  194.9 52.9 all-gather.4
  282.7 70.8 reduce-scatter.4
where the time goes:
time: 371 us
  waiting for transfers between devices  280 us (75%)
  matrix products  54.1 us (15%)
  between operations  14 us (4%)
  other arithmetic  10.3 us (3%)
  local copies, waits for them, and re-layouts  7.92 us (2%)
  starting transfers between devices  5.03 us (1%)
    reduce_scatter x1, waiting for transfers between devices, per_device(): lax.psum_scatter(contract(part, spikes, 0, 1), 'dp', scatter_dimension=0,...  98.5 us
    reduce_scatter x1, waiting for transfers between devices, per_device(): lax.psum_scatter((contract(gate_part, gate_grad, 1, 1) + contract(up_part...  66.4 us
    all_gather x1, waiting for transfers between devices, per_device(): piece = lax.all_gather(layer_input, 'dp', axis=1, tiled=True)  54.1 us
    dot_general x6, matrix products, contract(): lax.dot_general(left, right, (((left_dim,), (right_dim,)), ((), ())), pre...  54.1 us
    all_gather x1, waiting for transfers between devices, per_device(): piece = lax.all_gather(grad_block, 'dp', axis=1, tiled=True)  52.9 us
  transfers between devices with their start and end apart: 6, of which 5 were waited for; matrix products, arithmetic and copies ran while one was open for 2% of the time, Pallas kernels for 0%

commit v1 on v0

v1 whole, which is shorter than its diff:
```python
import functools

import jax
import jax.numpy as jnp
from jax import lax
from jax.experimental import pallas as pl
from jax.experimental.pallas import tpu as pltpu
from jax.sharding import PartitionSpec as P

decay_rate = 0.9
level_unit = 0.125
f32 = jnp.float32
bf16 = jnp.bfloat16
VMEM_LIMIT = 16 * 1024 * 1024


def in_vmem(x):
    return pltpu.with_memory_space_constraint(x, pltpu.VMEM)


def call(kernel, outs, *args, places=None, aliases=None):
    specs = []
    given = []
    for a in args:
        if a.dtype == jnp.int32 and a.ndim == 1:
            specs.append(pl.BlockSpec(memory_space=pltpu.SMEM))
            given.append(a)
        else:
            specs.append(pl.BlockSpec(memory_space=pltpu.VMEM))
            given.append(in_vmem(a))
    return pl.pallas_call(
        kernel,
        out_shape=[pltpu.VMEM(shape, dtype) for shape, dtype in outs],
        in_specs=specs,
        out_specs=[pl.BlockSpec(memory_space=pltpu.VMEM)] * len(outs),
        input_output_aliases=aliases or {},
        compiler_params=pltpu.CompilerParams(vmem_limit_bytes=VMEM_LIMIT),
    )(*given)


def nn(left, right):
    return lax.dot_general(left, right, (((1,), (0,)), ((), ())), preferred_element_type=f32)


def nt(left, right):
    return lax.dot_general(left, right, (((1,), (1,)), ((), ())), preferred_element_type=f32)


def tiles(total, width):
    width = min(width, total)
    return [slice(k, k + width) for k in range(0, total, width)]


def levels(threshold_ref, width_ref, at):
    threshold = level_unit * threshold_ref[:, at].astype(f32)
    scale = 1.0 / (level_unit * width_ref[:, at].astype(f32))
    return threshold, scale


def spikes_of(currents, threshold, scale):
    potential = None
    out = []
    for current in currents:
        if potential is None:
            potential = current
        else:
            potential = decay_rate * (potential - threshold * out[-1]) + current
        out.append(jax.nn.sigmoid((potential - threshold) * scale))
    return out


def spikes_back(spikes, cotangents, threshold, scale):
    after = None
    grads = [None] * len(spikes)
    for t in reversed(range(len(spikes))):
        slope = spikes[t] * (1.0 - spikes[t]) * scale
        if after is None:
            after = cotangents[t] * slope
        else:
            after = (cotangents[t] - decay_rate * threshold * after) * slope + decay_rate * after
        grads[t] = after
    return grads


def step_rows(count, tokens):
    return [slice(t * tokens, (t + 1) * tokens) for t in range(count)]


def whole_pieces(refs, shape):
    out = []
    pending = None
    for ref in refs:
        if ref.shape == shape:
            out.append(ref[...])
        elif pending is None:
            pending = ref[...]
        else:
            out.append(jnp.concatenate([pending, ref[...]], axis=0))
            pending = None
    return out


def gate_up_kernel(n_pieces, first, last, steps, tokens, *refs):
    at, refs = refs[0], list(refs[1:])
    piece_refs, refs = refs[:n_pieces], refs[n_pieces:]
    gate_w, up_w = refs[:2]
    refs = refs[2:]
    if not first:
        acc = refs[:2]
        refs = refs[2:]
    if last:
        threshold_ref, width_ref = refs[:2]
        refs = refs[2:]
    gate_out, up_out = refs[:2]
    rows = steps * tokens
    local = next(r.shape[1] for r in piece_refs)
    pieces = whole_pieces(piece_refs, (rows, local))
    left = jnp.concatenate(pieces, axis=1)
    for cols in tiles(gate_out.shape[1], 256):
        both = []
        for which, weight in enumerate((gate_w, up_w)):
            right = jnp.concatenate(
                [weight[pl.ds(pl.multiple_of(at[p], local), local), cols] for p in range(len(pieces))],
                axis=0,
            )
            total = nn(left, right)
            if not first:
                total = total + acc[which][:, cols]
            both.append(total)
            (gate_out, up_out)[which][:, cols] = total
        if last:
            threshold, scale = levels(threshold_ref, width_ref, cols)
            hidden = both[0] * jax.nn.sigmoid(both[0]) * both[1]
            parts = [hidden[r] for r in step_rows(steps, tokens)]
            out = spikes_of(parts, threshold, scale)
            refs[2][:, cols] = jnp.concatenate(out, axis=0).astype(bf16)


def down_kernel(n_own, n_blocks, at, spikes, down, *outs):
    left = spikes[...]
    for p in range(n_blocks):
        out = outs[p]
        local = out.shape[1]
        right = down[:, pl.ds(pl.multiple_of(at[p], local), local)]
        out[...] = nn(left, right).astype(out.dtype)


def out_kernel(steps, tokens, own, sib, fw, bw, x, cot, threshold_ref, width_ref, emitted, grad, grad16):
    threshold, scale = levels(threshold_ref, width_ref, slice(None))
    current = (
        own[...] + sib[...].astype(f32) + fw[...].astype(f32) + bw[...].astype(f32) + x[...].astype(f32)
    )
    rows = step_rows(steps, tokens)
    out = spikes_of([current[r] for r in rows], threshold, scale)
    emitted[...] = jnp.concatenate(out, axis=0).astype(bf16)
    grads = spikes_back(out, [cot[r, :].astype(f32) for r in rows], threshold, scale)
    total = jnp.concatenate(grads, axis=0)
    grad[...] = total
    grad16[...] = total.astype(bf16)


def spike_grad_kernel(n_pieces, first, last, steps, tokens, *refs):
    at, refs = refs[0], list(refs[1:])
    piece_refs, refs = refs[:n_pieces], refs[n_pieces:]
    down = refs[0]
    refs = refs[1:]
    if not first:
        acc = refs[0]
        refs = refs[1:]
    if last:
        gate, up, threshold_ref, width_ref = refs[:4]
        refs = refs[4:]
    rows = steps * tokens
    local = next(r.shape[1] for r in piece_refs)
    pieces = whole_pieces(piece_refs, (rows, local))
    left = jnp.concatenate(pieces, axis=1)
    for hid in tiles(down.shape[0], 256):
        right = jnp.concatenate(
            [down[hid, pl.ds(pl.multiple_of(at[p], local), local)] for p in range(len(pieces))], axis=1
        )
        total = nt(left, right)
        if not first:
            total = total + acc[:, hid]
        if not last:
            refs[0][:, hid] = total
            continue
        threshold, scale = levels(threshold_ref, width_ref, hid)
        gate_in, up_in = gate[:, hid], up[:, hid]
        sig = jax.nn.sigmoid(gate_in)
        act = gate_in * sig
        hidden = act * up_in
        parts = step_rows(steps, tokens)
        out = spikes_of([hidden[r] for r in parts], threshold, scale)
        grads = spikes_back(out, [total[r] for r in parts], threshold, scale)
        grad = jnp.concatenate(grads, axis=0)
        refs[0][:, hid] = (grad * up_in * (sig * (1.0 + gate_in * (1.0 - sig)))).astype(bf16)
        refs[1][:, hid] = (grad * act).astype(bf16)


def input_grad_kernel(n_blocks, at, gate_grad, up_grad, gate_w, up_w, *outs):
    left = jnp.concatenate([gate_grad[...], up_grad[...]], axis=1)
    for p in range(n_blocks):
        out = outs[p]
        local = out.shape[1]
        here = pl.ds(pl.multiple_of(at[p], local), local)
        right = jnp.concatenate([gate_w[here, :], up_w[here, :]], axis=1)
        out[...] = nt(left, right).astype(out.dtype)


def per_device(
    devices,
    layer_input,
    gate_weight,
    up_weight,
    down_weight,
    hidden_threshold,
    hidden_width,
    out_threshold,
    out_width,
    out_cotangent,
):
    local = layer_input.shape[1]
    steps = layer_input.shape[2]
    tokens = layer_input.shape[3]
    rows = steps * tokens
    half = rows // 2
    hid = gate_weight.shape[2]
    chips = devices // 2
    far = chips // 2
    side = chips // 2

    def chip_at(place):
        place = place % chips
        return jnp.where(place < side, 2 * place, 2 * (chips - 1 - place) + 1)

    order = [2 * p if p < side else 2 * (chips - 1 - p) + 1 for p in range(chips)]
    forward, backward, sibling = [], [], []
    for p in range(chips):
        a, b = order[p], order[(p + 1) % chips]
        for core in range(2):
            forward.append((2 * a + core, 2 * b + core))
            backward.append((2 * b + core, 2 * a + core))
            sibling.append((2 * a + core, 2 * a + 1 - core))
    send_fw = lambda v: lax.ppermute(v, "dp", forward)
    send_bw = lambda v: lax.ppermute(v, "dp", backward)
    swap = lambda v: lax.ppermute(v, "dp", sibling)

    index = lax.axis_index("dp").astype(jnp.int32)
    chip, core = index // 2, index % 2
    place = jnp.where(chip % 2 == 0, chip // 2, chips - 1 - chip // 2)

    def block_at(distance, sib):
        which = 2 * chip_at(place + distance) + (1 - core if sib else core)
        return which * local

    gate_w, up_w, down_w = gate_weight[0], up_weight[0], down_weight[0]
    x = jnp.transpose(layer_input[0], (1, 2, 0)).reshape(rows, local)
    cot = jnp.transpose(out_cotangent[0], (1, 2, 0)).reshape(rows, local)

    def gathered(mine):
        groups = [([mine, swap(mine)], [(0, False), (0, True)])]
        fw = bw = mine
        for k in range(1, far + 1):
            if k == far:
                fw, bw = fw[:half], bw[half:]
            fw, bw = send_fw(fw), send_bw(bw)
            if k < far:
                groups.append(
                    (
                        [fw, bw, swap(fw), swap(bw)],
                        [(-k, False), (k, False), (-k, True), (k, True)],
                    )
                )
            else:
                groups.append(([fw, bw, swap(fw), swap(bw)], [(-k, False), (-k, True)]))
        return groups

    def places(at):
        return jnp.stack([block_at(d, s) for d, s in at]).astype(jnp.int32)

    def scattered(blocks_of):
        own, sib = blocks_of([far])
        sib = [swap(s) for s in sib]
        total = own[0] + sib[0].astype(f32)
        fw, bw = total[:half].astype(bf16), total[half:].astype(bf16)
        for k in range(far - 1, 0, -1):
            fw, bw = send_fw(fw), send_bw(bw)
            own, sib = blocks_of([k, -k])
            sib = [swap(s) for s in sib]
            a, b = own[0] + sib[0].astype(f32), own[1] + sib[1].astype(f32)
            if k == far - 1:
                fw = jnp.concatenate([a[:half] + fw.astype(f32), a[half:]], axis=0).astype(bf16)
                bw = jnp.concatenate([b[:half], b[half:] + bw.astype(f32)], axis=0).astype(bf16)
            else:
                fw, bw = (a + fw.astype(f32)).astype(bf16), (b + bw.astype(f32)).astype(bf16)
        fw, bw = send_fw(fw), send_bw(bw)
        own, sib = blocks_of([0])
        return own[0], swap(sib[0]), fw, bw

    acc = None
    groups = gathered(x)
    hid_level, hid_spread = hidden_threshold, hidden_width
    for k, (pieces, at) in enumerate(groups):
        first, last = k == 0, k == len(groups) - 1
        args = [places(at), *pieces, gate_w, up_w]
        aliases = {}
        if not first:
            aliases = {len(args): 0, len(args) + 1: 1}
            args += list(acc)
        outs = [((rows, hid), f32)] * 2
        if last:
            args += [hid_level, hid_spread]
            outs = outs + [((rows, hid), bf16)]
        res = call(
            functools.partial(gate_up_kernel, len(pieces), first, last, steps, tokens),
            outs,
            *args,
            aliases=aliases,
        )
        acc = res[:2]
    gate, upward, spikes = res

    def down_blocks(distances):
        at = [(d, s) for s in (False, True) for d in distances]
        outs = [((rows, local), bf16 if s else f32) for _, s in at]
        res = call(
            functools.partial(down_kernel, len(distances), len(at)), outs, places(at), spikes, down_w
        )
        return res[: len(distances)], res[len(distances) :]

    own, sib, fw, bw = scattered(down_blocks)
    emitted, current_grad, grad16 = call(
        functools.partial(out_kernel, steps, tokens),
        [((rows, local), bf16), ((rows, local), f32), ((rows, local), bf16)],
        own, sib, fw, bw, x, cot, out_threshold, out_width,
    )

    acc = None
    groups = gathered(grad16)
    for k, (pieces, at) in enumerate(groups):
        first, last = k == 0, k == len(groups) - 1
        args = [places(at), *pieces, down_w]
        aliases = {}
        if not first:
            if not last:
                aliases = {len(args): 0}
            args += [acc]
        outs = [((rows, hid), f32)]
        if last:
            args += [gate, upward, hid_level, hid_spread]
            outs = [((rows, hid), bf16)] * 2
        res = call(
            functools.partial(spike_grad_kernel, len(pieces), first, last, steps, tokens),
            outs,
            *args,
            aliases=aliases,
        )
        acc = res[0]
    gate_grad, up_grad = res

    def input_blocks(distances):
        at = [(d, s) for s in (False, True) for d in distances]
        outs = [((rows, local), bf16 if s else f32) for _, s in at]
        res = call(
            functools.partial(input_grad_kernel, len(at)),
            outs, places(at), gate_grad, up_grad, gate_w, up_w,
        )
        return res[: len(distances)], res[len(distances) :]

    own, sib, fw, bw = scattered(input_blocks)
    input_grad = (
        own + sib.astype(f32) + fw.astype(f32) + bw.astype(f32) + current_grad
    ).astype(bf16)

    sections = lax.axis_size("section")
    incoming = lax.ppermute(emitted, "section", [(s, s + 1) for s in range(sections - 1)])
    returned = lax.ppermute(input_grad, "section", [(s + 1, s) for s in range(sections - 1)])

    def viewed(v):
        return jnp.transpose(v.reshape(steps, tokens, local), (2, 0, 1))[None]

    return viewed(incoming), viewed(returned)


def solution(mesh):
    placed = (
        P("section", "dp", None, None),
        P("section", None, "dp"),
        P("section", None, "dp"),
        P("section", "dp", None),
        P("section", "dp"),
        P("section", "dp"),
        P("section", "dp"),
        P("section", "dp"),
        P("section", "dp", None, None),
    )
    return jax.shard_map(
        functools.partial(per_device, mesh.shape["dp"]),
        mesh=mesh,
        in_specs=placed,
        out_specs=(P("section", "dp", None, None), P("section", "dp", None, None)),
        check_vma=False,
    )
```

time: 371 us -> 202 us (0.54)
  waiting for transfers between devices: 280 us -> 69.2 us
  matrix products: 54.1 us -> 0 us
  Pallas kernels: 0 us -> 48.6 us
  starting transfers between devices: 5.03 us -> 46.9 us
  local copies, waits for them, and re-layouts: 7.92 us -> 31.9 us
  between operations: 14 us -> 1.38 us
  other arithmetic: 10.3 us -> 3.45 us
    reduce_scatter x2 -> x0, waiting for transfers between devices: 165 us -> none  [the longest x1 98.5 us: per_device(): lax.psum_scatter(contract(part, spikes, 0, 1), 'dp', scatter_dimension=0,...]
    all_gather x2 -> x0, waiting for transfers between devices: 107 us -> none  [the longest x1 54.1 us: per_device(): piece = lax.all_gather(layer_input, 'dp', axis=1, tiled=True)]
    ppermute x2 -> x68, waiting for transfers between devices: 6.96 us -> 69.2 us  [the longest x16 44 us: per_device(): send_fw = lambda v: lax.ppermute(v, 'dp', forward)]
    dot_general x6 -> x0, matrix products: 54.1 us -> none  [contract(): lax.dot_general(left, right, (((left_dim,), (right_dim,)), ((), ())), pre...]
    pallas_call x0 -> x21, Pallas kernels: none -> 48.6 us  [call(): pl.pallas_call(kernel, out_shape=[pltpu.VMEM(shape, dtype) for shape, dty...]
    ppermute x2 -> x68, starting transfers between devices: 4.69 us -> 46.9 us  [the longest x16 27.3 us: per_device(): send_fw = lambda v: lax.ppermute(v, 'dp', forward)]
    unnamed x46 -> x74, local copies, waits for them, and re-layouts: 4.61 us -> 27.9 us
  transfers between devices with their start and end apart: 6 -> 68, of which waited for: 5 -> 24; matrix products, arithmetic and copies ran while one was open for 2% -> 3% of each run, Pallas kernels for 0% -> 18%
where the time goes in v1:
time: 202 us; the launch traced here: 201 us
  waiting for transfers between devices  69.2 us (34%)
  Pallas kernels  48.6 us (24%)
  starting transfers between devices  46.9 us (23%)
  local copies, waits for them, and re-layouts  31.9 us (16%)
  other arithmetic  3.45 us (2%)
    pallas_call x21, Pallas kernels, call(): pl.pallas_call(kernel, out_shape=[pltpu.VMEM(shape, dtype) for shape, dty...  48.6 us
    ppermute x16, waiting for transfers between devices, per_device(): send_fw = lambda v: lax.ppermute(v, 'dp', forward)  44 us
    unnamed x74, local copies, waits for them, and re-layouts  27.9 us
    ppermute x16, starting transfers between devices, per_device(): send_fw = lambda v: lax.ppermute(v, 'dp', forward)  27.3 us
    ppermute x16, waiting for transfers between devices, per_device(): send_bw = lambda v: lax.ppermute(v, 'dp', backward)  19 us
    ppermute x16, starting transfers between devices, per_device(): send_bw = lambda v: lax.ppermute(v, 'dp', backward)  7.73 us
    ppermute x34, starting transfers between devices, per_device(): swap = lambda v: lax.ppermute(v, 'dp', sibling)  7.11 us
    ppermute x1, waiting for transfers between devices, per_device(): lax.ppermute(input_grad, 'section', [(s + 1, s) for s in range(sections -...  6.09 us
  transfers between devices with their start and end apart: 68, of which 24 were waited for; matrix products, arithmetic and copies ran while one was open for 3% of the time, Pallas kernels for 18%

profile of v1, /device:TPU:0, one launch (start us, length us, event | category | flops | bytes accessed | tf_op | source)
XLA Modules:
  0.0 201.5 jit_solution(17414863247785743354)
XLA Ops:
  1.7 3.1 %collective-permute-start = (bf16[512,256]{1,0:T(8,128)(2,1)S(1)}, bf16[512,256]{1,0:T(8,128)(2,1)S(1)}, u32[]{:S(2)}, u32[]{:S(2)}) collective-permute-start(bf16[512,256]{1,0:T(8,128)(2,1)S(1)} %bitcast.75), channel_id=1, source_target_pairs={{0,4},{1,5},{4,8},{5,9},{8,12},{9,13},{12,14},{13,15},{14,10},{15,... | collective-permute-start | bytes 786440 | tf_op jit(solution)/shard_map/ppermute | solution.py:244
  4.8 6.2 %collective-permute-done.refs_1_ = bf16[512,256]{1,0:T(8,128)(2,1)S(1)} collective-permute-done((bf16[512,256]{1,0:T(8,128)(2,1)S(1)}, bf16[512,256]{1,0:T(8,128)(2,1)S(1)}, u32[]{:S(2)}, u32[]{:S(2)}) %collective-permute-start) | collective-permute-done | bytes 262176 | tf_op jit(solution)/shard_map/ppermute | solution.py:244
  13.1 5.5 %collective-permute-done.1.refs_1_ = bf16[512,256]{1,0:T(8,128)(2,1)S(1)} collective-permute-done((bf16[512,256]{1,0:T(8,128)(2,1)S(1)}, bf16[512,256]{1,0:T(8,128)(2,1)S(1)}, u32[]{:S(2)}, u32[]{:S(2)}) %collective-permute-start.1) | collective-permute-done | bytes 262176 | tf_op jit(solution)/shard_map/ppermute | solution.py:244
  21.1 4.1 %collective-permute-done.2.refs_1_ = bf16[512,256]{1,0:T(8,128)(2,1)S(1)} collective-permute-done((bf16[512,256]{1,0:T(8,128)(2,1)S(1)}, bf16[512,256]{1,0:T(8,128)(2,1)S(1)}, u32[]{:S(2)}, u32[]{:S(2)}) %collective-permute-start.2) | collective-permute-done | bytes 262176 | tf_op jit(solution)/shard_map/ppermute | solution.py:244
  33.5 3.4 %copy-done = bf16[1,4096,1024]{2,1,0:T(8,128)(2,1)S(1)} copy-done((bf16[1,4096,1024]{2,1,0:T(8,128)(2,1)S(1)}, bf16[1,4096,1024]{2,1,0:T(8,128)(2,1)}, u32[]{:S(2)}) %copy-start) | copy-done | bytes 8388632
  36.9 3.4 %copy-done.2 = bf16[1,4096,1024]{2,1,0:T(8,128)(2,1)S(1)} copy-done((bf16[1,4096,1024]{2,1,0:T(8,128)(2,1)S(1)}, bf16[1,4096,1024]{2,1,0:T(8,128)(2,1)}, u32[]{:S(2)}) %copy-start.2) | copy-done | bytes 8388632
  44.6 2.4 %copy-done.3 = bf16[1,4096,1024]{2,1,0:T(8,128)(2,1)S(1)} copy-done((bf16[1,4096,1024]{2,1,0:T(8,128)(2,1)S(1)}, bf16[1,4096,1024]{2,1,0:T(8,128)(2,1)}, u32[]{:S(2)}) %copy-start.3) | copy-done | bytes 8388632
  48.9 3.1 %shard_map.105 = (f32[512,1024]{1,0:T(8,128)S(1)}, f32[512,1024]{1,0:T(8,128)S(1)}) custom-call(s32[4]{0:T(128)S(1)} %pad_add_fusion.4.refs_0_, bf16[512,256]{1,0:T(8,128)(2,1)S(1)} %copy-done.12, bf16[512,256]{1,0:T(8,128)(2,1)S(1)} %copy-done.14, bf16[512,256]{1,0:T(8,128)(2,1)S(1)} %copy-done.20, ...), custom_call_target="tpu_custom_call", output_to_operand_aliasing={{0}: (7, {}), {1}: (8, {})} | custom-call | tf_op jit(solution)/shard_map/pallas_call | solution.py:31
  52.1 3.6 %shard_map.106 = (f32[512,1024]{1,0:T(8,128)S(1)}, f32[512,1024]{1,0:T(8,128)S(1)}) custom-call(s32[4]{0:T(128)S(1)} %pad_add_fusion.3.refs_0_, bf16[512,256]{1,0:T(8,128)(2,1)S(1)} %collective-permute-done.1.refs_1_, bf16[512,256]{1,0:T(8,128)(2,1)} %collective-permute-done.5.refs_2_, ...), custom_call_target="tpu_custom_call", output_to_operand_aliasing={{0}: (7, {}), {1}: (8, {})} | custom-call | tf_op jit(solution)/shard_map/pallas_call | solution.py:31
  55.7 3.6 %shard_map.107 = (f32[512,1024]{1,0:T(8,128)S(1)}, f32[512,1024]{1,0:T(8,128)S(1)}) custom-call(s32[4]{0:T(128)S(1)} %pad_add_fusion.2.refs_0_, bf16[512,256]{1,0:T(8,128)(2,1)S(1)} %collective-permute-done.2.refs_1_, bf16[512,256]{1,0:T(8,128)(2,1)S(1)} %collective-permute-done.6.refs_2_, ...), custom_call_target="tpu_custom_call", output_to_operand_aliasing={{0}: (7, {}), {1}: (8, {})} | custom-call | tf_op jit(solution)/shard_map/pallas_call | solution.py:31
  62.3 3.6 %shard_map.108 = (f32[512,1024]{1,0:T(8,128)S(1)}, f32[512,1024]{1,0:T(8,128)S(1)}, bf16[512,1024]{1,0:T(8,128)(2,1)S(1)}) custom-call(s32[2]{0:T(128)S(1)} %pad_add_fusion.1.refs_0_, bf16[256,256]{1,0:T(8,128)(2,1)S(1)} %collective-permute-done.3.refs_1_, ...), custom_call_target="tpu_custom_call", output_to_operand_aliasing={{0}: (7, {}), {1}: (8, {})} | custom-call | tf_op jit(solution)/shard_map/pallas_call | solution.py:31
  76.4 3.2 %collective-permute-done.29 = bf16[256,256]{1,0:T(8,128)(2,1)S(1)} collective-permute-done((bf16[256,256]{1,0:T(8,128)(2,1)S(1)}, bf16[256,256]{1,0:T(8,128)(2,1)S(1)}, u32[]{:S(2)}, u32[]{:S(2)}) %collective-permute-start.29) | collective-permute-done | bytes 131104 | tf_op jit(solution)/shard_map/ppermute | solution.py:245
  84.6 2.7 %collective-permute-done.30 = bf16[512,256]{1,0:T(8,128)(2,1)S(1)} collective-permute-done((bf16[512,256]{1,0:T(8,128)(2,1)S(1)}, bf16[512,256]{1,0:T(8,128)(2,1)S(1)}, u32[]{:S(2)}, u32[]{:S(2)}) %collective-permute-start.30) | collective-permute-done | bytes 262176 | tf_op jit(solution)/shard_map/ppermute | solution.py:245
  89.5 2.0 shard_map.109
  91.5 2.4 %collective-permute-done.31 = bf16[512,256]{1,0:T(8,128)(2,1)S(1)} collective-permute-done((bf16[512,256]{1,0:T(8,128)(2,1)S(1)}, bf16[512,256]{1,0:T(8,128)(2,1)S(1)}, u32[]{:S(2)}, u32[]{:S(2)}) %collective-permute-start.31) | collective-permute-done | bytes 262176 | tf_op jit(solution)/shard_map/ppermute | solution.py:245
  98.6 2.6 %collective-permute-done.32.bw = bf16[512,256]{1,0:T(8,128)(2,1)S(1)} collective-permute-done((bf16[512,256]{1,0:T(8,128)(2,1)}, bf16[512,256]{1,0:T(8,128)(2,1)S(1)}, u32[]{:S(2)}, u32[]{:S(2)}) %collective-permute-start.32) | collective-permute-done | bytes 262176 | tf_op jit(solution)/shard_map/ppermute | solution.py:245
  108.1 6.0 %collective-permute-done.34.refs_1_ = bf16[512,256]{1,0:T(8,128)(2,1)S(1)} collective-permute-done((bf16[512,256]{1,0:T(8,128)(2,1)S(1)}, bf16[512,256]{1,0:T(8,128)(2,1)S(1)}, u32[]{:S(2)}, u32[]{:S(2)}) %collective-permute-start.34) | collective-permute-done | bytes 262176 | tf_op jit(solution)/shard_map/ppermute | solution.py:244
  116.3 6.6 %collective-permute-done.35.refs_1_ = bf16[512,256]{1,0:T(8,128)(2,1)S(1)} collective-permute-done((bf16[512,256]{1,0:T(8,128)(2,1)S(1)}, bf16[512,256]{1,0:T(8,128)(2,1)S(1)}, u32[]{:S(2)}, u32[]{:S(2)}) %collective-permute-start.35) | collective-permute-done | bytes 262176 | tf_op jit(solution)/shard_map/ppermute | solution.py:244
  125.9 3.5 %collective-permute-done.36.refs_1_ = bf16[512,256]{1,0:T(8,128)(2,1)S(1)} collective-permute-done((bf16[512,256]{1,0:T(8,128)(2,1)S(1)}, bf16[512,256]{1,0:T(8,128)(2,1)S(1)}, u32[]{:S(2)}, u32[]{:S(2)}) %collective-permute-start.36) | collective-permute-done | bytes 262176 | tf_op jit(solution)/shard_map/ppermute | solution.py:244
  133.8 3.4 %collective-permute-done.37.refs_1_ = bf16[256,256]{1,0:T(8,128)(2,1)S(1)} collective-permute-done((bf16[256,256]{1,0:T(8,128)(2,1)S(1)}, bf16[256,256]{1,0:T(8,128)(2,1)S(1)}, u32[]{:S(2)}, u32[]{:S(2)}) %collective-permute-start.37) | collective-permute-done | bytes 131104 | tf_op jit(solution)/shard_map/ppermute | solution.py:244
  139.0 3.4 %copy-done.4 = bf16[1,1024,4096]{2,1,0:T(8,128)(2,1)S(1)} copy-done((bf16[1,1024,4096]{2,1,0:T(8,128)(2,1)S(1)}, bf16[1,1024,4096]{2,1,0:T(8,128)(2,1)}, u32[]{:S(2)}) %copy-start.4) | copy-done | bytes 8388632
  143.7 2.0 shard_map.116.refs_6_
  145.7 1.9 shard_map.117.refs_6_
  147.7 2.0 shard_map.118.refs_6_
  151.2 3.3 %shard_map.119 = (bf16[512,1024]{1,0:T(8,128)(2,1)S(1)}, bf16[512,1024]{1,0:T(8,128)(2,1)S(1)}) custom-call(s32[2]{0:T(128)S(1)} %pad_add_fusion.1.refs_0_, bf16[256,256]{1,0:T(8,128)(2,1)S(1)} %collective-permute-done.37.refs_1_, bf16[256,256]{1,0:T(8,128)(2,1)S(1)} %collective-permute-done.41.refs_2_, ...), custom_call_target="tpu_custom_call" | custom-call | tf_op jit(solution)/shard_map/pallas_call | solution.py:31
  157.2 2.9 %shard_map.123 = (f32[512,256]{1,0:T(8,128)S(1)}, f32[512,256]{1,0:T(8,128)S(1)}, bf16[512,256]{1,0:T(8,128)(2,1)S(1)}, bf16[512,256]{1,0:T(8,128)(2,1)S(1)}) custom-call(s32[4]{0:T(128)S(1)} %pad_add_fusion.7.at, bf16[512,1024]{1,0:T(8,128)(2,1)S(1)} %get-tuple-element.79.gate_grad, bf16[512,1024]{1,0:T(8,128)(2,1)S(1)} %get-tuple-element.80.up_grad, ...), custom_call_target="tpu_custom_call" | custom-call | tf_op jit(solution)/shard_map/pallas_call | solution.py:31
  160.1 2.9 %shard_map.122 = (f32[512,256]{1,0:T(8,128)S(1)}, f32[512,256]{1,0:T(8,128)S(1)}, bf16[512,256]{1,0:T(8,128)(2,1)S(1)}, bf16[512,256]{1,0:T(8,128)(2,1)S(1)}) custom-call(s32[4]{0:T(128)S(1)} %pad_add_fusion.6.at, bf16[512,1024]{1,0:T(8,128)(2,1)S(1)} %get-tuple-element.79.gate_grad, bf16[512,1024]{1,0:T(8,128)(2,1)S(1)} %get-tuple-element.80.up_grad, ...), custom_call_target="tpu_custom_call" | custom-call | tf_op jit(solution)/shard_map/pallas_call | solution.py:31
  166.7 3.0 %collective-permute-done.56 = bf16[256,256]{1,0:T(8,128)(2,1)S(1)} collective-permute-done((bf16[256,256]{1,0:T(8,128)(2,1)S(1)}, bf16[256,256]{1,0:T(8,128)(2,1)S(1)}, u32[]{:S(2)}, u32[]{:S(2)}) %collective-permute-start.56) | collective-permute-done | bytes 131104 | tf_op jit(solution)/shard_map/ppermute | solution.py:244
  172.0 2.9 %shard_map.121 = (f32[512,256]{1,0:T(8,128)S(1)}, f32[512,256]{1,0:T(8,128)S(1)}, bf16[512,256]{1,0:T(8,128)(2,1)S(1)}, bf16[512,256]{1,0:T(8,128)(2,1)S(1)}) custom-call(s32[4]{0:T(128)S(1)} %pad_add_fusion.5.at, bf16[512,1024]{1,0:T(8,128)(2,1)S(1)} %get-tuple-element.79.gate_grad, bf16[512,1024]{1,0:T(8,128)(2,1)S(1)} %get-tuple-element.80.up_grad, ...), custom_call_target="tpu_custom_call" | custom-call | tf_op jit(solution)/shard_map/pallas_call | solution.py:31
  181.5 2.4 %collective-permute-done.58 = bf16[512,256]{1,0:T(8,128)(2,1)S(1)} collective-permute-done((bf16[512,256]{1,0:T(8,128)(2,1)S(1)}, bf16[512,256]{1,0:T(8,128)(2,1)S(1)}, u32[]{:S(2)}, u32[]{:S(2)}) %collective-permute-start.58) | collective-permute-done | bytes 262176 | tf_op jit(solution)/shard_map/ppermute | solution.py:244
  186.3 3.4 %collective-permute-start.33 = (bf16[512,256]{1,0:T(8,128)(2,1)S(1)}, bf16[512,256]{1,0:T(8,128)(2,1)S(1)}, u32[]{:S(2)}, u32[]{:S(2)}) collective-permute-start(bf16[512,256]{1,0:T(8,128)(2,1)S(1)} %get-tuple-element.75), channel_id=1, source_target_pairs={{0,16},{1,17},{2,18},{3,19},{4,20},{5,21},{6,22},{7,23},{8,24},{9,... | collective-permute-start | bytes 786440 | tf_op jit(solution)/shard_map/ppermute | solution.py:376
  194.5 6.1 %collective-permute-done.67 = bf16[512,256]{1,0:T(8,128)(2,1)S(1)} collective-permute-done((bf16[512,256]{1,0:T(8,128)(2,1)S(1)}, bf16[512,256]{1,0:T(8,128)(2,1)S(1)}, u32[]{:S(2)}, u32[]{:S(2)}) %collective-permute-start.67) | collective-permute-done | bytes 262176 | tf_op jit(solution)/shard_map/ppermute | solution.py:377
  (249 shorter events, 89.7 us)
Async XLA Ops:
  1.7 9.3 %collective-permute-start = (bf16[512,256]{1,0:T(8,128)(2,1)S(1)}, bf16[512,256]{1,0:T(8,128)(2,1)S(1)}, u32[]{:S(2)}, u32[]{:S(2)}) collective-permute-start(bf16[512,256]{1,0:T(8,128)(2,1)S(1)} %bitcast.75), channel_id=1, source_target_pairs={{0,4},{1,5},{4,8},{5,9},{8,12},{9,13},{12,14},{13,15},{14,10},{15,... | collective-permute-start | bytes 786440 | tf_op jit(solution)/shard_map/ppermute | solution.py:244
  4.8 8.1 %collective-permute-start.4 = (bf16[512,256]{1,0:T(8,128)(2,1)S(1)}, bf16[512,256]{1,0:T(8,128)(2,1)S(1)}, u32[]{:S(2)}, u32[]{:S(2)}) collective-permute-start(bf16[512,256]{1,0:T(8,128)(2,1)S(1)} %bitcast.76), channel_id=1, source_target_pairs={{4,0},{5,1},{8,4},{9,5},{12,8},{13,9},{14,12},{15,13},{10,14},{11,... | collective-permute-start | bytes 786440 | tf_op jit(solution)/shard_map/ppermute | solution.py:245
  20.6 7.7 %collective-permute-start.16 = (bf16[512,256]{1,0:T(8,128)(2,1)S(1)}, bf16[512,256]{1,0:T(8,128)(2,1)S(1)}, u32[]{:S(2)}, u32[]{:S(2)}) collective-permute-start(bf16[512,256]{1,0:T(8,128)(2,1)S(1)} %bitcast.77), channel_id=1, source_target_pairs={{0,1},{1,0},{4,5},{5,4},{8,9},{9,8},{12,13},{13,12},{14,15},{15,14... | collective-permute-start | bytes 786440 | tf_op jit(solution)/shard_map/ppermute | solution.py:246
  20.6 8.3 %collective-permute-start.14 = (bf16[512,256]{1,0:T(8,128)(2,1)S(1)}, bf16[512,256]{1,0:T(8,128)(2,1)S(1)}, u32[]{:S(2)}, u32[]{:S(2)}) collective-permute-start(bf16[512,256]{1,0:T(8,128)(2,1)S(1)} %collective-permute-done.refs_1_), channel_id=1, source_target_pairs={{0,1},{1,0},{4,5},{5,4},{8,9},{9,8},{12,13},{13,12},{14,15},{15,14... | collective-permute-start | bytes 786440 | tf_op jit(solution)/shard_map/ppermute | solution.py:246
  21.1 8.4 %collective-permute-start.15 = (bf16[512,256]{1,0:T(8,128)(2,1)S(1)}, bf16[512,256]{1,0:T(8,128)(2,1)S(1)}, u32[]{:S(2)}, u32[]{:S(2)}) collective-permute-start(bf16[512,256]{1,0:T(8,128)(2,1)S(1)} %collective-permute-done.4.refs_2_), channel_id=1, source_target_pairs={{0,1},{1,0},{4,5},{5,4},{8,9},{9,8},{12,13},{13,12},{14,15},{15,14... | collective-permute-start | bytes 786440 | tf_op jit(solution)/shard_map/ppermute | solution.py:246
  29.5 22.5 %collective-permute-start.13 = (bf16[512,256]{1,0:T(8,128)(2,1)}, bf16[512,256]{1,0:T(8,128)(2,1)}, u32[]{:S(2)}, u32[]{:S(2)}) collective-permute-start(bf16[512,256]{1,0:T(8,128)(2,1)} %collective-permute-done.5.refs_2_), channel_id=1, source_target_pairs={{0,1},{1,0},{4,5},{5,4},{8,9},{9,8},{12,13},{13,12},{14,15},{15,14... | collective-permute-start | bytes 786440 | tf_op jit(solution)/shard_map/ppermute | solution.py:246
  30.2 25.4 %collective-permute-start.10 = (bf16[512,256]{1,0:T(8,128)(2,1)S(1)}, bf16[512,256]{1,0:T(8,128)(2,1)}, u32[]{:S(2)}, u32[]{:S(2)}) collective-permute-start(bf16[512,256]{1,0:T(8,128)(2,1)S(1)} %collective-permute-done.2.refs_1_), channel_id=1, source_target_pairs={{0,1},{1,0},{4,5},{5,4},{8,9},{9,8},{12,13},{13,12},{14,15},{15,14... | collective-permute-start | bytes 786440 | tf_op jit(solution)/shard_map/ppermute | solution.py:246
  31.4 24.2 %collective-permute-start.11 = (bf16[512,256]{1,0:T(8,128)(2,1)S(1)}, bf16[512,256]{1,0:T(8,128)(2,1)}, u32[]{:S(2)}, u32[]{:S(2)}) collective-permute-start(bf16[512,256]{1,0:T(8,128)(2,1)S(1)} %collective-permute-done.6.refs_2_), channel_id=1, source_target_pairs={{0,1},{1,0},{4,5},{5,4},{8,9},{9,8},{12,13},{13,12},{14,15},{15,14... | collective-permute-start | bytes 786440 | tf_op jit(solution)/shard_map/ppermute | solution.py:246
  31.6 29.0 %collective-permute-start.8 = (bf16[256,256]{1,0:T(8,128)(2,1)S(1)}, bf16[256,256]{1,0:T(8,128)(2,1)}, u32[]{:S(2)}, u32[]{:S(2)}) collective-permute-start(bf16[256,256]{1,0:T(8,128)(2,1)S(1)} %collective-permute-done.3.refs_1_), channel_id=1, source_target_pairs={{0,1},{1,0},{4,5},{5,4},{8,9},{9,8},{12,13},{13,12},{14,15},{15,14... | collective-permute-start | bytes 393224 | tf_op jit(solution)/shard_map/ppermute | solution.py:246
  33.4 27.2 %collective-permute-start.9 = (bf16[256,256]{1,0:T(8,128)(2,1)}, bf16[256,256]{1,0:T(8,128)(2,1)}, u32[]{:S(2)}, u32[]{:S(2)}) collective-permute-start(bf16[256,256]{1,0:T(8,128)(2,1)} %collective-permute-done.7.refs_2_), channel_id=1, source_target_pairs={{0,1},{1,0},{4,5},{5,4},{8,9},{9,8},{12,13},{13,12},{14,15},{15,14... | collective-permute-start | bytes 393224 | tf_op jit(solution)/shard_map/ppermute | solution.py:246
  73.0 11.1 %collective-permute-start.27 = (bf16[512,256]{1,0:T(8,128)(2,1)S(1)}, bf16[512,256]{1,0:T(8,128)(2,1)S(1)}, u32[]{:S(2)}, u32[]{:S(2)}) collective-permute-start(bf16[512,256]{1,0:T(8,128)(2,1)S(1)} %get-tuple-element.72), channel_id=1, source_target_pairs={{0,1},{1,0},{4,5},{5,4},{8,9},{9,8},{12,13},{13,12},{14,15},{15,14... | collective-permute-start | bytes 786440 | tf_op jit(solution)/shard_map/ppermute | solution.py:246
  73.5 14.3 %collective-permute-start.19 = (bf16[512,256]{1,0:T(8,128)(2,1)S(1)}, bf16[512,256]{1,0:T(8,128)(2,1)S(1)}, u32[]{:S(2)}, u32[]{:S(2)}) collective-permute-start(bf16[512,256]{1,0:T(8,128)(2,1)S(1)} %get-tuple-element.64), channel_id=1, source_target_pairs={{0,1},{1,0},{4,5},{5,4},{8,9},{9,8},{12,13},{13,12},{14,15},{15,14... | collective-permute-start | bytes 786440 | tf_op jit(solution)/shard_map/ppermute | solution.py:246
  79.7 7.5 %collective-permute-start.30 = (bf16[512,256]{1,0:T(8,128)(2,1)S(1)}, bf16[512,256]{1,0:T(8,128)(2,1)S(1)}, u32[]{:S(2)}, u32[]{:S(2)}) collective-permute-start(bf16[512,256]{1,0:T(8,128)(2,1)S(1)} %pad_maximum_fusion.1), channel_id=1, source_target_pairs={{4,0},{5,1},{8,4},{9,5},{12,8},{13,9},{14,12},{15,13},{10,14},{11,... | collective-permute-start | bytes 786440 | tf_op jit(solution)/shard_map/ppermute | solution.py:245
  80.3 7.5 %collective-permute-start.23 = (bf16[512,256]{1,0:T(8,128)(2,1)S(1)}, bf16[512,256]{1,0:T(8,128)(2,1)S(1)}, u32[]{:S(2)}, u32[]{:S(2)}) collective-permute-start(bf16[512,256]{1,0:T(8,128)(2,1)S(1)} %pad_maximum_fusion), channel_id=1, source_target_pairs={{0,4},{1,5},{4,8},{5,9},{8,12},{9,13},{12,14},{13,15},{14,10},{15,... | collective-permute-start | bytes 786440 | tf_op jit(solution)/shard_map/ppermute | solution.py:244
  84.0 7.5 %collective-permute-start.26 = (bf16[512,256]{1,0:T(8,128)(2,1)S(1)}, bf16[512,256]{1,0:T(8,128)(2,1)S(1)}, u32[]{:S(2)}, u32[]{:S(2)}) collective-permute-start(bf16[512,256]{1,0:T(8,128)(2,1)S(1)} %get-tuple-element.70), channel_id=1, source_target_pairs={{0,1},{1,0},{4,5},{5,4},{8,9},{9,8},{12,13},{13,12},{14,15},{15,14... | collective-permute-start | bytes 786440 | tf_op jit(solution)/shard_map/ppermute | solution.py:246
  84.1 11.1 %collective-permute-start.18 = (bf16[512,256]{1,0:T(8,128)(2,1)S(1)}, bf16[512,256]{1,0:T(8,128)(2,1)S(1)}, u32[]{:S(2)}, u32[]{:S(2)}) collective-permute-start(bf16[512,256]{1,0:T(8,128)(2,1)S(1)} %get-tuple-element.62), channel_id=1, source_target_pairs={{0,1},{1,0},{4,5},{5,4},{8,9},{9,8},{12,13},{13,12},{14,15},{15,14... | collective-permute-start | bytes 786440 | tf_op jit(solution)/shard_map/ppermute | solution.py:246
  106.0 8.1 %collective-permute-start.34 = (bf16[512,256]{1,0:T(8,128)(2,1)S(1)}, bf16[512,256]{1,0:T(8,128)(2,1)S(1)}, u32[]{:S(2)}, u32[]{:S(2)}) collective-permute-start(bf16[512,256]{1,0:T(8,128)(2,1)S(1)} %get-tuple-element.76.refs_1_), channel_id=1, source_target_pairs={{0,4},{1,5},{4,8},{5,9},{8,12},{9,13},{12,14},{13,15},{14,10},{15,... | collective-permute-start | bytes 786440 | tf_op jit(solution)/shard_map/ppermute | solution.py:244
  107.6 8.0 %collective-permute-start.38 = (bf16[512,256]{1,0:T(8,128)(2,1)S(1)}, bf16[512,256]{1,0:T(8,128)(2,1)S(1)}, u32[]{:S(2)}, u32[]{:S(2)}) collective-permute-start(bf16[512,256]{1,0:T(8,128)(2,1)S(1)} %get-tuple-element.76.refs_1_), channel_id=1, source_target_pairs={{4,0},{5,1},{8,4},{9,5},{12,8},{13,9},{14,12},{15,13},{10,14},{11,... | collective-permute-start | bytes 786440 | tf_op jit(solution)/shard_map/ppermute | solution.py:245
  114.1 8.9 %collective-permute-start.35 = (bf16[512,256]{1,0:T(8,128)(2,1)S(1)}, bf16[512,256]{1,0:T(8,128)(2,1)S(1)}, u32[]{:S(2)}, u32[]{:S(2)}) collective-permute-start(bf16[512,256]{1,0:T(8,128)(2,1)S(1)} %collective-permute-done.34.refs_1_), channel_id=1, source_target_pairs={{0,4},{1,5},{4,8},{5,9},{8,12},{9,13},{12,14},{13,15},{14,10},{15,... | collective-permute-start | bytes 786440 | tf_op jit(solution)/shard_map/ppermute | solution.py:244
  115.7 9.1 %collective-permute-start.39 = (bf16[512,256]{1,0:T(8,128)(2,1)S(1)}, bf16[512,256]{1,0:T(8,128)(2,1)S(1)}, u32[]{:S(2)}, u32[]{:S(2)}) collective-permute-start(bf16[512,256]{1,0:T(8,128)(2,1)S(1)} %collective-permute-done.38.refs_2_), channel_id=1, source_target_pairs={{4,0},{5,1},{8,4},{9,5},{12,8},{13,9},{14,12},{15,13},{10,14},{11,... | collective-permute-start | bytes 786440 | tf_op jit(solution)/shard_map/ppermute | solution.py:245
  125.4 7.5 %collective-permute-start.48 = (bf16[512,256]{1,0:T(8,128)(2,1)S(1)}, bf16[512,256]{1,0:T(8,128)(2,1)S(1)}, u32[]{:S(2)}, u32[]{:S(2)}) collective-permute-start(bf16[512,256]{1,0:T(8,128)(2,1)S(1)} %collective-permute-done.34.refs_1_), channel_id=1, source_target_pairs={{0,1},{1,0},{4,5},{5,4},{8,9},{9,8},{12,13},{13,12},{14,15},{15,14... | collective-permute-start | bytes 786440 | tf_op jit(solution)/shard_map/ppermute | solution.py:246
  131.2 14.5 %collective-permute-start.47 = (bf16[512,256]{1,0:T(8,128)(2,1)S(1)}, bf16[512,256]{1,0:T(8,128)(2,1)S(1)}, u32[]{:S(2)}, u32[]{:S(2)}) collective-permute-start(bf16[512,256]{1,0:T(8,128)(2,1)S(1)} %collective-permute-done.39.refs_2_), channel_id=1, source_target_pairs={{0,1},{1,0},{4,5},{5,4},{8,9},{9,8},{12,13},{13,12},{14,15},{15,14... | collective-permute-start | bytes 786440 | tf_op jit(solution)/shard_map/ppermute | solution.py:246
  132.9 14.8 %collective-permute-start.44 = (bf16[512,256]{1,0:T(8,128)(2,1)S(1)}, bf16[512,256]{1,0:T(8,128)(2,1)S(1)}, u32[]{:S(2)}, u32[]{:S(2)}) collective-permute-start(bf16[512,256]{1,0:T(8,128)(2,1)S(1)} %collective-permute-done.36.refs_1_), channel_id=1, source_target_pairs={{0,1},{1,0},{4,5},{5,4},{8,9},{9,8},{12,13},{13,12},{14,15},{15,14... | collective-permute-start | bytes 786440 | tf_op jit(solution)/shard_map/ppermute | solution.py:246
  133.1 14.6 %collective-permute-start.45 = (bf16[512,256]{1,0:T(8,128)(2,1)S(1)}, bf16[512,256]{1,0:T(8,128)(2,1)S(1)}, u32[]{:S(2)}, u32[]{:S(2)}) collective-permute-start(bf16[512,256]{1,0:T(8,128)(2,1)S(1)} %collective-permute-done.40.refs_2_), channel_id=1, source_target_pairs={{0,1},{1,0},{4,5},{5,4},{8,9},{9,8},{12,13},{13,12},{14,15},{15,14... | collective-permute-start | bytes 786440 | tf_op jit(solution)/shard_map/ppermute | solution.py:246
  137.2 12.5 %collective-permute-start.42 = (bf16[256,256]{1,0:T(8,128)(2,1)S(1)}, bf16[256,256]{1,0:T(8,128)(2,1)S(1)}, u32[]{:S(2)}, u32[]{:S(2)}) collective-permute-start(bf16[256,256]{1,0:T(8,128)(2,1)S(1)} %collective-permute-done.37.refs_1_), channel_id=1, source_target_pairs={{0,1},{1,0},{4,5},{5,4},{8,9},{9,8},{12,13},{13,12},{14,15},{15,14... | collective-permute-start | bytes 393224 | tf_op jit(solution)/shard_map/ppermute | solution.py:246
  139.0 10.7 %collective-permute-start.43 = (bf16[256,256]{1,0:T(8,128)(2,1)S(1)}, bf16[256,256]{1,0:T(8,128)(2,1)S(1)}, u32[]{:S(2)}, u32[]{:S(2)}) collective-permute-start(bf16[256,256]{1,0:T(8,128)(2,1)S(1)} %collective-permute-done.41.refs_2_), channel_id=1, source_target_pairs={{0,1},{1,0},{4,5},{5,4},{8,9},{9,8},{12,13},{13,12},{14,15},{15,14... | collective-permute-start | bytes 393224 | tf_op jit(solution)/shard_map/ppermute | solution.py:246
  163.1 11.9 %collective-permute-start.53 = (bf16[512,256]{1,0:T(8,128)(2,1)S(1)}, bf16[512,256]{1,0:T(8,128)(2,1)S(1)}, u32[]{:S(2)}, u32[]{:S(2)}) collective-permute-start(bf16[512,256]{1,0:T(8,128)(2,1)S(1)} %get-tuple-element.86), channel_id=1, source_target_pairs={{0,1},{1,0},{4,5},{5,4},{8,9},{9,8},{12,13},{13,12},{14,15},{15,14... | collective-permute-start | bytes 786440 | tf_op jit(solution)/shard_map/ppermute | solution.py:246
  163.6 15.4 %collective-permute-start.61 = (bf16[512,256]{1,0:T(8,128)(2,1)S(1)}, bf16[512,256]{1,0:T(8,128)(2,1)S(1)}, u32[]{:S(2)}, u32[]{:S(2)}) collective-permute-start(bf16[512,256]{1,0:T(8,128)(2,1)S(1)} %get-tuple-element.94), channel_id=1, source_target_pairs={{0,1},{1,0},{4,5},{5,4},{8,9},{9,8},{12,13},{13,12},{14,15},{15,14... | collective-permute-start | bytes 786440 | tf_op jit(solution)/shard_map/ppermute | solution.py:246
  171.4 7.5 %collective-permute-start.64 = (bf16[512,256]{1,0:T(8,128)(2,1)S(1)}, bf16[512,256]{1,0:T(8,128)(2,1)S(1)}, u32[]{:S(2)}, u32[]{:S(2)}) collective-permute-start(bf16[512,256]{1,0:T(8,128)(2,1)S(1)} %pad_maximum_fusion.3), channel_id=1, source_target_pairs={{4,0},{5,1},{8,4},{9,5},{12,8},{13,9},{14,12},{15,13},{10,14},{11,... | collective-permute-start | bytes 786440 | tf_op jit(solution)/shard_map/ppermute | solution.py:245
  175.0 10.7 %collective-permute-start.60 = (bf16[512,256]{1,0:T(8,128)(2,1)S(1)}, bf16[512,256]{1,0:T(8,128)(2,1)S(1)}, u32[]{:S(2)}, u32[]{:S(2)}) collective-permute-start(bf16[512,256]{1,0:T(8,128)(2,1)S(1)} %get-tuple-element.92), channel_id=1, source_target_pairs={{0,1},{1,0},{4,5},{5,4},{8,9},{9,8},{12,13},{13,12},{14,15},{15,14... | collective-permute-start | bytes 786440 | tf_op jit(solution)/shard_map/ppermute | solution.py:246
  181.4 8.3 %collective-permute-start.51 = (bf16[512,256]{1,0:T(8,128)(2,1)S(1)}, bf16[512,256]{1,0:T(8,128)(2,1)S(1)}, u32[]{:S(2)}, u32[]{:S(2)}) collective-permute-start(bf16[512,256]{1,0:T(8,128)(2,1)S(1)} %get-tuple-element.82), channel_id=1, source_target_pairs={{0,1},{1,0},{4,5},{5,4},{8,9},{9,8},{12,13},{13,12},{14,15},{15,14... | collective-permute-start | bytes 786440 | tf_op jit(solution)/shard_map/ppermute | solution.py:246
  192.3 8.3 %collective-permute-start.67 = (bf16[512,256]{1,0:T(8,128)(2,1)S(1)}, bf16[512,256]{1,0:T(8,128)(2,1)S(1)}, u32[]{:S(2)}, u32[]{:S(2)}) collective-permute-start(bf16[512,256]{1,0:T(8,128)(2,1)S(1)} %add_convert_fusion), channel_id=1, source_target_pairs={{16,0},{17,1},{18,2},{19,3},{20,4},{21,5},{22,6},{23,7},{24,8},{25... | collective-permute-start | bytes 786440 | tf_op jit(solution)/shard_map/ppermute | solution.py:377
  (73 other events, 393.2 us)

commit v2 on v1

--- a/solution.py
+++ b/solution.py
@@ -11,14 +11,14 @@
 level_unit = 0.125
 f32 = jnp.float32
 bf16 = jnp.bfloat16
-VMEM_LIMIT = 16 * 1024 * 1024
+VMEM_LIMIT = 8 * 1024 * 1024
 
 
 def in_vmem(x):
     return pltpu.with_memory_space_constraint(x, pltpu.VMEM)
 
 
-def call(kernel, outs, *args, places=None, aliases=None):
+def call(kernel, outs, *args, flops=0, aliases=None, fetch=()):
     specs = []
     given = []
     for a in args:
@@ -28,14 +28,59 @@
         else:
             specs.append(pl.BlockSpec(memory_space=pltpu.VMEM))
             given.append(in_vmem(a))
-    return pl.pallas_call(
-        kernel,
+    outs = list(outs)
+    n_in, n_out, n_slabs, n_copies = len(args), len(outs), 0, 0
+    for at, axis, local, weights in fetch:
+        specs += [pl.BlockSpec(memory_space=pltpu.SMEM)] + [pl.BlockSpec(memory_space=pltpu.HBM)] * len(weights)
+        given += [at] + [pltpu.with_memory_space_constraint(w, pltpu.HBM) for w in weights]
+        for w in weights:
+            size = at.shape[0] * local
+            outs.append(((size, w.shape[1]) if axis == 0 else (w.shape[0], size), w.dtype))
+        n_slabs += len(weights)
+        n_copies += len(weights) * at.shape[0]
+
+    def body(*refs):
+        ins, refs = refs[:n_in], refs[n_in:]
+        asked = []
+        for at, axis, local, weights in fetch:
+            asked.append((refs[0], refs[1 : 1 + len(weights)]))
+            refs = refs[1 + len(weights) :]
+        slabs = list(refs[n_out : n_out + n_slabs])
+        copies = []
+        for (at, axis, local, weights), (at_ref, sources) in zip(fetch, asked):
+            mine, slabs = slabs[: len(weights)], slabs[len(weights) :]
+            for p in range(at.shape[0]):
+                here = pl.ds(pl.multiple_of(at_ref[p], local), local)
+                there = slice(p * local, (p + 1) * local)
+                for source, slab in zip(sources, mine):
+                    pair = (
+                        (source.at[here, :], slab.at[there, :])
+                        if axis == 0
+                        else (source.at[:, here], slab.at[:, there])
+                    )
+                    copies.append(pltpu.make_async_copy(*pair, refs[n_out + n_slabs].at[len(copies)]))
+        for copy in copies:
+            copy.start()
+        if kernel is not None:
+            kernel(*ins, *refs[:n_out])
+        for copy in copies:
+            copy.wait()
+
+    res = pl.pallas_call(
+        body,
         out_shape=[pltpu.VMEM(shape, dtype) for shape, dtype in outs],
         in_specs=specs,
         out_specs=[pl.BlockSpec(memory_space=pltpu.VMEM)] * len(outs),
+        scratch_shapes=[pltpu.SemaphoreType.DMA((n_copies,))] if n_copies else [],
         input_output_aliases=aliases or {},
         compiler_params=pltpu.CompilerParams(vmem_limit_bytes=VMEM_LIMIT),
+        cost_estimate=pl.CostEstimate(flops=flops, bytes_accessed=flops // 512, transcendentals=0),
     )(*given)
+    slabs, got = list(res[n_out:]), []
+    for _, _, _, weights in fetch:
+        got.append(slabs[: len(weights)])
+        slabs = slabs[len(weights) :]
+    return list(res[:n_out]), got
 
 
 def nn(left, right):
@@ -80,6 +125,10 @@
             after = (cotangents[t] - decay_rate * threshold * after) * slope + decay_rate * after
         grads[t] = after
     return grads
+
+
+def tied(value, after):
+    return value if after is None else lax.optimization_barrier((value, after))[0]
 
 
 def step_rows(count, tokens):
@@ -101,33 +150,24 @@
 
 
 def gate_up_kernel(n_pieces, first, last, steps, tokens, *refs):
-    at, refs = refs[0], list(refs[1:])
+    refs = list(refs)
     piece_refs, refs = refs[:n_pieces], refs[n_pieces:]
-    gate_w, up_w = refs[:2]
-    refs = refs[2:]
+    slabs, refs = refs[:2], refs[2:]
     if not first:
-        acc = refs[:2]
-        refs = refs[2:]
+        acc, refs = refs[:2], refs[2:]
     if last:
         threshold_ref, width_ref = refs[:2]
         refs = refs[2:]
-    gate_out, up_out = refs[:2]
-    rows = steps * tokens
-    local = next(r.shape[1] for r in piece_refs)
-    pieces = whole_pieces(piece_refs, (rows, local))
-    left = jnp.concatenate(pieces, axis=1)
-    for cols in tiles(gate_out.shape[1], 256):
+    local = piece_refs[0].shape[1]
+    left = jnp.concatenate(whole_pieces(piece_refs, (steps * tokens, local)), axis=1)
+    for cols in tiles(refs[0].shape[1], 256):
         both = []
-        for which, weight in enumerate((gate_w, up_w)):
-            right = jnp.concatenate(
-                [weight[pl.ds(pl.multiple_of(at[p], local), local), cols] for p in range(len(pieces))],
-                axis=0,
-            )
-            total = nn(left, right)
+        for which in range(2):
+            total = nn(left, slabs[which][:, cols])
             if not first:
                 total = total + acc[which][:, cols]
             both.append(total)
-            (gate_out, up_out)[which][:, cols] = total
+            refs[which][:, cols] = total
         if last:
             threshold, scale = levels(threshold_ref, width_ref, cols)
             hidden = both[0] * jax.nn.sigmoid(both[0]) * both[1]
@@ -136,13 +176,11 @@
             refs[2][:, cols] = jnp.concatenate(out, axis=0).astype(bf16)
 
 
-def down_kernel(n_own, n_blocks, at, spikes, down, *outs):
+def down_kernel(spikes, slab, *outs):
     left = spikes[...]
-    for p in range(n_blocks):
-        out = outs[p]
+    for p, out in enumerate(outs):
         local = out.shape[1]
-        right = down[:, pl.ds(pl.multiple_of(at[p], local), local)]
-        out[...] = nn(left, right).astype(out.dtype)
+        out[...] = nn(left, slab[:, p * local : (p + 1) * local]).astype(out.dtype)
 
 
 def out_kernel(steps, tokens, own, sib, fw, bw, x, cot, threshold_ref, width_ref, emitted, grad, grad16):
@@ -160,25 +198,18 @@
 
 
 def spike_grad_kernel(n_pieces, first, last, steps, tokens, *refs):
-    at, refs = refs[0], list(refs[1:])
+    refs = list(refs)
     piece_refs, refs = refs[:n_pieces], refs[n_pieces:]
-    down = refs[0]
-    refs = refs[1:]
+    slab, refs = refs[0], refs[1:]
     if not first:
-        acc = refs[0]
-        refs = refs[1:]
+        acc, refs = refs[0], refs[1:]
     if last:
         gate, up, threshold_ref, width_ref = refs[:4]
         refs = refs[4:]
-    rows = steps * tokens
-    local = next(r.shape[1] for r in piece_refs)
-    pieces = whole_pieces(piece_refs, (rows, local))
-    left = jnp.concatenate(pieces, axis=1)
-    for hid in tiles(down.shape[0], 256):
-        right = jnp.concatenate(
-            [down[hid, pl.ds(pl.multiple_of(at[p], local), local)] for p in range(len(pieces))], axis=1
-        )
-        total = nt(left, right)
+    local = piece_refs[0].shape[1]
+    left = jnp.concatenate(whole_pieces(piece_refs, (steps * tokens, local)), axis=1)
+    for hid in tiles(slab.shape[0], 256):
+        total = nt(left, slab[hid, :])
         if not first:
             total = total + acc[:, hid]
         if not last:
@@ -197,13 +228,12 @@
         refs[1][:, hid] = (grad * act).astype(bf16)
 
 
-def input_grad_kernel(n_blocks, at, gate_grad, up_grad, gate_w, up_w, *outs):
+def input_grad_kernel(gate_grad, up_grad, gate_slab, up_slab, *outs):
     left = jnp.concatenate([gate_grad[...], up_grad[...]], axis=1)
-    for p in range(n_blocks):
-        out = outs[p]
+    for p, out in enumerate(outs):
         local = out.shape[1]
-        here = pl.ds(pl.multiple_of(at[p], local), local)
-        right = jnp.concatenate([gate_w[here, :], up_w[here, :]], axis=1)
+        here = slice(p * local, (p + 1) * local)
+        right = jnp.concatenate([gate_slab[here, :], up_slab[here, :]], axis=1)
         out[...] = nt(left, right).astype(out.dtype)
 
 
@@ -253,119 +283,164 @@
         which = 2 * chip_at(place + distance) + (1 - core if sib else core)
         return which * local
 
-    gate_w, up_w, down_w = gate_weight[0], up_weight[0], down_weight[0]
     x = jnp.transpose(layer_input[0], (1, 2, 0)).reshape(rows, local)
     cot = jnp.transpose(out_cotangent[0], (1, 2, 0)).reshape(rows, local)
 
-    def gathered(mine):
-        groups = [([mine, swap(mine)], [(0, False), (0, True)])]
+    def with_sibling(distances):
+        return [(d, s) for s in (False, True) for d in distances]
+
+    come = [[0]] + [[-k, k] for k in range(1, far)] + [[-far]]
+    gathers = [
+        [(d, False) for d in now] + [(d, True) for d in before]
+        for now, before in zip(come + [[]], [[]] + come)
+    ]
+    scatters = [with_sibling(g) for g in [[far]] + [[k, -k] for k in range(far - 1, 0, -1)] + [[0]]]
+    gate_up = (0, local, (gate_weight[0], up_weight[0]))
+    down = (1, local, (down_weight[0],))
+    phases = ((gathers, gate_up), (scatters, down), (gathers, down), (scatters, gate_up))
+    wanted = {(f, k): (g, *w) for f, (gs, w) in enumerate(phases) for k, g in enumerate(gs)}
+    end = far + 1
+    brought_by = {(0, 0): [(0, 1), (0, 2)], (1, far): [(2, 0), (2, 1)], (2, 0): [(2, 2), (2, 3)]}
+    for k in range(1, far):
+        brought_by[0, k] = [(0, k + 2)]
+        brought_by[2, k] = [(2, k + 3)] if k + 3 <= end else []
+    brought_by[0, far - 2] = [(0, far), (0, end)]
+    brought_by[0, far - 1] = [(1, 0), (1, 1)]
+    brought_by[2, far - 2] = [(2, far), (2, end), (3, 0)]
+    if far > 2:
+        brought_by[2, far - 1] = [(3, 1)]
+    held_slabs = {}
+
+    def bring(which, after=None):
+        group, axis, size, weights = wanted[which]
+        at = jnp.stack([block_at(d, s) for d, s in group]).astype(jnp.int32)
+        return (tied(at, after), axis, size, weights)
+
+    def run(which, kernel, outs, *args, after=None, **kwargs):
+        if which not in held_slabs:
+            held_slabs[which] = call(None, [], fetch=[bring(which, after)])[1][0]
+        given = []
+        for a in args:
+            given += held_slabs[which] if a is None else [a]
+        later = brought_by.get(which, [])
+        if which[0] in (1, 3) and 1 <= which[1] < far and (which[0], which[1] + 1) not in later:
+            later = later + [(which[0], which[1] + 1)]
+        later = [w for w in later if w not in held_slabs]
+        res, got = call(kernel, outs, *given, fetch=[bring(w, after) for w in later], **kwargs)
+        held_slabs.update(zip(later, got))
+        return res
+
+    def gathered(mine, take):
+        own, sib, held = [mine], [], None
         fw = bw = mine
         for k in range(1, far + 1):
-            if k == far:
-                fw, bw = fw[:half], bw[half:]
+            sent = (fw[:half], bw[half:]) if k == far else (fw, bw)
+            fw, bw = send_fw(sent[0]), send_bw(sent[1])
+            swaps = [swap(v) for v in own]
+            held = take(own + sib, k - 1, held)
+            sib = swaps
+            fw, bw, held = lax.optimization_barrier((fw, bw, held))
+            own = [fw, bw]
+        swaps = [swap(v) for v in own]
+        held = take(own + sib, far, held)
+        return take(swaps, far + 1, held)
+
+    def scattered(blocks_of):
+        def summed(blocks, swaps):
+            return [o + s.astype(f32) for o, s in zip(blocks[0], swaps)]
+
+        now = blocks_of(0, None)
+        swaps = [swap(v) for v in now[1]]
+        later = blocks_of(1, None)
+        now, swaps, later = lax.optimization_barrier((now, swaps, later))
+        total = summed(now, swaps)[0]
+        fw, bw = total[:half].astype(bf16), total[half:].astype(bf16)
+        for k in range(1, far):
+            after = fw
             fw, bw = send_fw(fw), send_bw(bw)
-            if k < far:
-                groups.append(
-                    (
-                        [fw, bw, swap(fw), swap(bw)],
-                        [(-k, False), (k, False), (-k, True), (k, True)],
-                    )
-                )
-            else:
-                groups.append(([fw, bw, swap(fw), swap(bw)], [(-k, False), (-k, True)]))
-        return groups
-
-    def places(at):
-        return jnp.stack([block_at(d, s) for d, s in at]).astype(jnp.int32)
-
-    def scattered(blocks_of):
-        own, sib = blocks_of([far])
-        sib = [swap(s) for s in sib]
-        total = own[0] + sib[0].astype(f32)
-        fw, bw = total[:half].astype(bf16), total[half:].astype(bf16)
-        for k in range(far - 1, 0, -1):
-            fw, bw = send_fw(fw), send_bw(bw)
-            own, sib = blocks_of([k, -k])
-            sib = [swap(s) for s in sib]
-            a, b = own[0] + sib[0].astype(f32), own[1] + sib[1].astype(f32)
-            if k == far - 1:
+            now = later
+            swaps = [swap(v) for v in now[1]]
+            later = blocks_of(k + 1, after)
+            fw, bw, later = lax.optimization_barrier((fw, bw, later))
+            a, b = summed(now, swaps)
+            if k == 1:
                 fw = jnp.concatenate([a[:half] + fw.astype(f32), a[half:]], axis=0).astype(bf16)
                 bw = jnp.concatenate([b[:half], b[half:] + bw.astype(f32)], axis=0).astype(bf16)
             else:
                 fw, bw = (a + fw.astype(f32)).astype(bf16), (b + bw.astype(f32)).astype(bf16)
         fw, bw = send_fw(fw), send_bw(bw)
-        own, sib = blocks_of([0])
-        return own[0], swap(sib[0]), fw, bw
-
-    acc = None
-    groups = gathered(x)
+        return later[0][0], swap(later[1][0]), fw, bw
+
     hid_level, hid_spread = hidden_threshold, hidden_width
-    for k, (pieces, at) in enumerate(groups):
-        first, last = k == 0, k == len(groups) - 1
-        args = [places(at), *pieces, gate_w, up_w]
+
+    def take_inputs(pieces, k, acc):
+        first, last = k == 0, k == end
+        args = [*pieces, None]
         aliases = {}
         if not first:
-            aliases = {len(args): 0, len(args) + 1: 1}
+            aliases = {len(pieces) + 2: 0, len(pieces) + 3: 1}
             args += list(acc)
         outs = [((rows, hid), f32)] * 2
         if last:
             args += [hid_level, hid_spread]
             outs = outs + [((rows, hid), bf16)]
-        res = call(
+        return run(
+            (0, k),
             functools.partial(gate_up_kernel, len(pieces), first, last, steps, tokens),
             outs,
             *args,
+            flops=4 * rows * hid * local * len(gathers[k]),
             aliases=aliases,
+            after=x if first else None,
         )
-        acc = res[:2]
-    gate, upward, spikes = res
-
-    def down_blocks(distances):
-        at = [(d, s) for s in (False, True) for d in distances]
-        outs = [((rows, local), bf16 if s else f32) for _, s in at]
-        res = call(
-            functools.partial(down_kernel, len(distances), len(at)), outs, places(at), spikes, down_w
+
+    gate, upward, spikes = gathered(x, take_inputs)
+
+    def down_blocks(k, after):
+        outs = [((rows, local), bf16 if s else f32) for _, s in scatters[k]]
+        res = run(
+            (1, k), down_kernel, outs, spikes, None,
+            flops=2 * rows * hid * local * len(outs), after=after,
         )
-        return res[: len(distances)], res[len(distances) :]
+        return res[: len(res) // 2], res[len(res) // 2 :]
 
     own, sib, fw, bw = scattered(down_blocks)
-    emitted, current_grad, grad16 = call(
+    (emitted, current_grad, grad16), _ = call(
         functools.partial(out_kernel, steps, tokens),
         [((rows, local), bf16), ((rows, local), f32), ((rows, local), bf16)],
         own, sib, fw, bw, x, cot, out_threshold, out_width,
     )
 
-    acc = None
-    groups = gathered(grad16)
-    for k, (pieces, at) in enumerate(groups):
-        first, last = k == 0, k == len(groups) - 1
-        args = [places(at), *pieces, down_w]
+    def take_grads(pieces, k, acc):
+        first, last = k == 0, k == end
+        args = [*pieces, None]
         aliases = {}
         if not first:
             if not last:
-                aliases = {len(args): 0}
-            args += [acc]
+                aliases = {len(pieces) + 1: 0}
+            args += acc
         outs = [((rows, hid), f32)]
         if last:
             args += [gate, upward, hid_level, hid_spread]
             outs = [((rows, hid), bf16)] * 2
-        res = call(
+        return run(
+            (2, k),
             functools.partial(spike_grad_kernel, len(pieces), first, last, steps, tokens),
             outs,
             *args,
+            flops=2 * rows * hid * local * len(gathers[k]),
             aliases=aliases,
         )
-        acc = res[0]
-    gate_grad, up_grad = res
-
-    def input_blocks(distances):
-        at = [(d, s) for s in (False, True) for d in distances]
-        outs = [((rows, local), bf16 if s else f32) for _, s in at]
-        res = call(
-            functools.partial(input_grad_kernel, len(at)),
-            outs, places(at), gate_grad, up_grad, gate_w, up_w,
+
+    gate_grad, up_grad = gathered(grad16, take_grads)
+
+    def input_blocks(k, after):
+        outs = [((rows, local), bf16 if s else f32) for _, s in scatters[k]]
+        res = run(
+            (3, k), input_grad_kernel, outs, gate_grad, up_grad, None,
+            flops=4 * rows * hid * local * len(outs), after=after,
         )
-        return res[: len(distances)], res[len(distances) :]
+        return res[: len(res) // 2], res[len(res) // 2 :]
 
     own, sib, fw, bw = scattered(input_blocks)
     input_grad = (

time: 202 us -> 166 us (0.82)
  waiting for transfers between devices: 69.2 us -> 38.1 us
  local copies, waits for them, and re-layouts: 31.9 us -> 7.61 us
  Pallas kernels: 48.6 us -> 68.4 us
    ppermute x16, waiting for transfers between devices: 44 us -> 8.12 us  [per_device(): send_fw = lambda v: lax.ppermute(v, 'dp', forward)]
    unnamed x74 -> x20, local copies, waits for them, and re-layouts: 27.9 us -> 3.53 us
    pallas_call x21 -> x24, Pallas kernels: 48.6 us -> 68.4 us  [call(): pl.pallas_call(body, out_shape=[pltpu.VMEM(shape, dtype) for shape, dtype...]
    ppermute x16, waiting for transfers between devices: 19 us -> 23.8 us  [per_device(): send_bw = lambda v: lax.ppermute(v, 'dp', backward)]
    ppermute x1, waiting for transfers between devices: 0.01 us -> 2.29 us  [per_device(): lax.ppermute(emitted, 'section', [(s, s + 1) for s in range(sections - 1)])]
    ppermute x1, waiting for transfers between devices: 6.09 us -> 3.81 us  [per_device(): lax.ppermute(input_grad, 'section', [(s + 1, s) for s in range(sections -...]
  transfers between devices with their start and end apart: 68 -> 68, of which waited for: 24 -> 25; matrix products, arithmetic and copies ran while one was open for 3% -> 3% of each run, Pallas kernels for 18% -> 37%
where the time goes in v2:
time: 166 us; the launch traced here: 165 us
  Pallas kernels  68.4 us (41%)
  starting transfers between devices  46.6 us (28%)
  waiting for transfers between devices  38.1 us (23%)
  local copies, waits for them, and re-layouts  7.61 us (5%)
  other arithmetic  3.49 us (2%)
    pallas_call x24, Pallas kernels, call(): pl.pallas_call(body, out_shape=[pltpu.VMEM(shape, dtype) for shape, dtype...  68.4 us
    ppermute x16, starting transfers between devices, per_device(): send_fw = lambda v: lax.ppermute(v, 'dp', forward)  25.7 us
    ppermute x16, waiting for transfers between devices, per_device(): send_bw = lambda v: lax.ppermute(v, 'dp', backward)  23.8 us
    ppermute x16, starting transfers between devices, per_device(): send_bw = lambda v: lax.ppermute(v, 'dp', backward)  8.73 us
    ppermute x16, waiting for transfers between devices, per_device(): send_fw = lambda v: lax.ppermute(v, 'dp', forward)  8.12 us
    ppermute x34, starting transfers between devices, per_device(): swap = lambda v: lax.ppermute(v, 'dp', sibling)  7.44 us
    ppermute x1, waiting for transfers between devices, per_device(): lax.ppermute(input_grad, 'section', [(s + 1, s) for s in range(sections -...  3.81 us
    unnamed x20, local copies, waits for them, and re-layouts  3.53 us
  transfers between devices with their start and end apart: 68, of which 25 were waited for; matrix products, arithmetic and copies ran while one was open for 3% of the time, Pallas kernels for 37%

profile of v2, /device:TPU:0, one launch (start us, length us, event | category | flops | bytes accessed | tf_op | source)
XLA Modules:
  0.0 165.5 jit_solution(14140292664675080079)
XLA Ops:
  1.7 3.1 %collective-permute-start = (bf16[512,256]{1,0:T(8,128)(2,1)S(1)}, bf16[512,256]{1,0:T(8,128)(2,1)S(1)}, u32[]{:S(2)}, u32[]{:S(2)}) collective-permute-start(bf16[512,256]{1,0:T(8,128)(2,1)S(1)} %bitcast.37), channel_id=1, source_target_pairs={{0,4},{1,5},{4,8},{5,9},{8,12},{9,13},{12,14},{13,15},{14,10},{15,... | collective-permute-start | bytes 786440 | tf_op jit(solution)/shard_map/ppermute | solution.py:274
  6.2 4.2 %shard_map.105 = (f32[512,1024]{1,0:T(8,128)S(1)}, f32[512,1024]{1,0:T(8,128)S(1)}, bf16[768,1024]{1,0:T(8,128)(2,1)S(1)}, bf16[768,1024]{1,0:T(8,128)(2,1)S(1)}...) custom-call(bf16[512,256]{1,0:T(8,128)(2,1)S(1)} %bitcast.40, ...), custom_call_target="tpu_custom_call" | custom-call | flops 536870912 | bytes 1048576 | tf_op jit(solution)/shard_map/pallas_call | solution.py:69
  15.2 4.4 %shard_map.106 = (f32[512,1024]{1,0:T(8,128)S(1)}, f32[512,1024]{1,0:T(8,128)S(1)}, bf16[1024,1024]{1,0:T(8,128)(2,1)S(1)}, bf16[1024,1024]{1,0:T(8,128)(2,1)S(1)}) custom-call(bf16[512,256]{1,0:T(8,128)(2,1)S(1)} %collective-permute-done.refs_0_, bf16[512,256]{1,0:T(8,128)(2,1)S(1)} %collective-permute-done.1.refs_1_, ...), custom_call_target="tpu_custom_call", output_to_operand_aliasing={{0}: (5, {}), {1}: (6, {})} | custom-call | flops 1610612736 | bytes 3145728 | tf_op jit(solution)/shard_map/pallas_call | solution.py:69
  23.6 4.8 %shard_map.107 = (f32[512,1024]{1,0:T(8,128)S(1)}, f32[512,1024]{1,0:T(8,128)S(1)}, bf16[768,1024]{1,0:T(8,128)(2,1)S(1)}, bf16[768,1024]{1,0:T(8,128)(2,1)S(1)}...) custom-call(bf16[512,256]{1,0:T(8,128)(2,1)S(1)} %collective-permute-, ...), custom_call_target="tpu_custom_call", output_to_operand_aliasing={{0}: (6, {}), {1}: (7, {})} | custom-call | flops 2147483648 | bytes 4194304 | tf_op jit(solution)/shard_map/pallas_call | solution.py:69
  32.0 4.9 %shard_map.108 = (f32[512,1024]{1,0:T(8,128)S(1)}, f32[512,1024]{1,0:T(8,128)S(1)}, bf16[1024,512]{1,0:T(8,128)(2,1)S(1)}, bf16[1024,1024]{1,0:T(8,128)(2,1)S(1)}) custom-call(bf16[512,256]{1,0:T(8,128)(2,1)S(1)} %collective-permute-done.5.refs_0_, ...), custom_call_target="tpu_custom_call", output_to_operand_aliasing={{0}: (6, {}), {1}: (7, {})} | custom-call | flops 2147483648 | bytes 4194304 | tf_op jit(solution)/shard_map/pallas_call | solution.py:69
  37.5 2.0 %shard_map.109 = (f32[512,1024]{1,0:T(8,128)S(1)}, f32[512,1024]{1,0:T(8,128)S(1)}) custom-call(bf16[256,256]{1,0:T(8,128)(2,1)S(1)} %collective-permute-done.9.refs_0_, bf16[256,256]{1,0:T(8,128)(2,1)S(1)} %collective-permute-done.10.refs_1_, bf16[512,256]{1,0:T(8,128)(2,1)S(1)} %collective-permute-done.15.refs_2_, ...), custom_call_target="tpu_custom_call", output_to_operand_aliasing={{0}: (6, {}), {1}: (7, {})} | custom-call | flops 1610612736 | bytes 3145728 | tf_op jit(solution)/shard_map/pallas_call | solution.py:69
  39.5 1.7 %shard_map.110 = (f32[512,1024]{1,0:T(8,128)S(1)}, f32[512,1024]{1,0:T(8,128)S(1)}, bf16[512,1024]{1,0:T(8,128)(2,1)S(1)}) custom-call(bf16[256,256]{1,0:T(8,128)(2,1)S(1)} %collective-permute-done.13.refs_0_, bf16[256,256]{1,0:T(8,128)(2,1)S(1)} %collective-permute-done.14.refs_1_, ...), custom_call_target="tpu_custom_call", output_to_operand_aliasing={{0}: (4, {}), {1}: (5, {})} | custom-call | flops 536870912 | bytes 1048576 | tf_op jit(solution)/shard_map/pallas_call | solution.py:69
  42.2 2.7 %shard_map.112 = (f32[512,256]{1,0:T(8,128)S(1)}, f32[512,256]{1,0:T(8,128)S(1)}, bf16[512,256]{1,0:T(8,128)(2,1)S(1)}, bf16[512,256]{1,0:T(8,128)(2,1)S(1)}, bf16[1024,1024]{1,0:T(8,128)(2,1)S(1)}) custom-call(bf16[512,1024]{1,0:T(8,128)(2,1)S(1)} %get-tuple-element.211.refs_0_, bf16[1024,1024]{1,0:T(8,128)(2,1)S(1)} %get-tuple-element.215.refs_1_, ...), custom_call_target="tpu_custom_call" | custom-call | flops 1073741824 | bytes 2097152 | tf_op jit(solution)/shard_map/pallas_call | solution.py:69
  45.5 1.8 %collective-permute-start.18 = (bf16[256,256]{1,0:T(8,128)(2,1)S(1)}, bf16[256,256]{1,0:T(8,128)(2,1)S(1)}, u32[]{:S(2)}, u32[]{:S(2)}) collective-permute-start(bf16[256,256]{1,0:T(8,128)(2,1)S(1)} %get-tuple-element.341), channel_id=1, source_target_pairs={{0,4},{1,5},{4,8},{5,9},{8,12},{9,13},{12,14},{13,15},{14,10},{15,... | collective-permute-start | bytes 393224 | tf_op jit(solution)/shard_map/ppermute | solution.py:274
  47.8 2.7 %shard_map.113 = (f32[512,256]{1,0:T(8,128)S(1)}, f32[512,256]{1,0:T(8,128)S(1)}, bf16[512,256]{1,0:T(8,128)(2,1)S(1)}, bf16[512,256]{1,0:T(8,128)(2,1)S(1)}, bf16[1024,1024]{1,0:T(8,128)(2,1)S(1)}) custom-call(bf16[512,1024]{1,0:T(8,128)(2,1)S(1)} %get-tuple-element.211.refs_0_, bf16[1024,1024]{1,0:T(8,128)(2,1)S(1)} %get-tuple-element.222.refs_1_, ...), custom_call_target="tpu_custom_call" | custom-call | flops 1073741824 | bytes 2097152 | tf_op jit(solution)/shard_map/pallas_call | solution.py:69
  53.3 1.6 collective-permute-start.22
  55.6 2.5 %shard_map.114 = (f32[512,256]{1,0:T(8,128)S(1)}, f32[512,256]{1,0:T(8,128)S(1)}, bf16[512,256]{1,0:T(8,128)(2,1)S(1)}, bf16[512,256]{1,0:T(8,128)(2,1)S(1)}, bf16[1024,512]{1,0:T(8,128)(2,1)S(1)}) custom-call(bf16[512,1024]{1,0:T(8,128)(2,1)S(1)} %get-tuple-element.211.refs_0_, bf16[1024,1024]{1,0:T(8,128)(2,1)S(1)} %get-tuple-element.236.refs_1_, ...), custom_call_target="tpu_custom_call" | custom-call | flops 1073741824 | bytes 2097152 | tf_op jit(solution)/shard_map/pallas_call | solution.py:69
  58.0 2.0 %collective-permute-done.24 = bf16[512,256]{1,0:T(8,128)(2,1)S(1)} collective-permute-done((bf16[512,256]{1,0:T(8,128)(2,1)S(1)}, bf16[512,256]{1,0:T(8,128)(2,1)S(1)}, u32[]{:S(2)}, u32[]{:S(2)}) %collective-permute-start.24) | collective-permute-done | bytes 262176 | tf_op jit(solution)/shard_map/ppermute | solution.py:275
  60.9 1.7 collective-permute-start.25
  63.1 3.2 %shard_map.115 = (f32[512,256]{1,0:T(8,128)S(1)}, bf16[512,256]{1,0:T(8,128)(2,1)}, bf16[1024,256]{1,0:T(8,128)(2,1)S(1)}, bf16[1024,768]{1,0:T(8,128)(2,1)S(1)}) custom-call(bf16[512,1024]{1,0:T(8,128)(2,1)S(1)} %get-tuple-element.211.refs_0_, bf16[1024,512]{1,0:T(8,128)(2,1)S(1)} %get-tuple-element.246.refs_1_, s32[1]{0:T(128)} %bitcast.3.refs_0_.refs_2_, ...), custom_call_target="tpu_custom_call" | custom-call | flops 536870912 | bytes 1048576 | tf_op jit(solution)/shard_map/pallas_call | solution.py:69
  73.0 4.5 %collective-permute-done.32.refs_3_ = bf16[512,256]{1,0:T(8,128)(2,1)S(1)} collective-permute-done((bf16[512,256]{1,0:T(8,128)(2,1)}, bf16[512,256]{1,0:T(8,128)(2,1)S(1)}, u32[]{:S(2)}, u32[]{:S(2)}) %collective-permute-start.32) | collective-permute-done | bytes 262176 | tf_op jit(solution)/shard_map/ppermute | solution.py:275
  81.1 1.7 collective-permute-start.34
  83.2 2.9 %shard_map.117 = (f32[512,1024]{1,0:T(8,128)S(1)}, bf16[1024,1024]{1,0:T(8,128)(2,1)S(1)}, bf16[1024,1024]{1,0:T(8,128)(2,1)S(1)}) custom-call(bf16[512,256]{1,0:T(8,128)(2,1)S(1)} %get-tuple-element.260.refs_0_, bf16[1024,256]{1,0:T(8,128)(2,1)S(1)} %get-tuple-element.261.refs_1_, s32[4]{0:T(128)S(1)} %get-tuple-element.174.refs_6_.refs_2_, ...), custom_call_target="tpu_custom_call" | custom-call | flops 268435456 | bytes 524288 | tf_op jit(solution)/shard_map/pallas_call | solution.py:69
  86.1 2.0 %collective-permute-done.34.refs_0_ = bf16[512,256]{1,0:T(8,128)(2,1)S(1)} collective-permute-done((bf16[512,256]{1,0:T(8,128)(2,1)S(1)}, bf16[512,256]{1,0:T(8,128)(2,1)S(1)}, u32[]{:S(2)}, u32[]{:S(2)}) %collective-permute-start.34) | collective-permute-done | bytes 262176 | tf_op jit(solution)/shard_map/ppermute | solution.py:274
  92.0 2.7 %shard_map.118 = (f32[512,1024]{1,0:T(8,128)S(1)}, bf16[1024,768]{1,0:T(8,128)(2,1)S(1)}) custom-call(bf16[512,256]{1,0:T(8,128)(2,1)S(1)} %collective-permute-done.34.refs_0_, bf16[512,256]{1,0:T(8,128)(2,1)S(1)} %collective-permute-done.35.refs_1_, bf16[512,256]{1,0:T(8,128)(2,1)S(1)} %collective-permute-done.38.refs_2_, ...), custom_call_target="tpu_custom_call", output_to_operand_aliasing={{0}: (4, {})} | custom-call | flops 805306368 | bytes 1572864 | tf_op jit(solution)/shard_map/pallas_call | solution.py:69
  100.0 3.4 %shard_map.119 = (f32[512,1024]{1,0:T(8,128)S(1)}, bf16[1024,256]{1,0:T(8,128)(2,1)S(1)}, bf16[512,1024]{1,0:T(8,128)(2,1)S(1)}, bf16[512,1024]{1,0:T(8,128)(2,1)S(1)}) custom-call(bf16[512,256]{1,0:T(8,128)(2,1)S(1)} %collective-permute-done.36.refs_0_, bf16[512,256]{1,0:T(8,128)(2,1)S(1)} %collective-permute-done.37.refs_1_, ...), custom_call_target="tpu_custom_call", output_to_operand_aliasing={{0}: (5, {})} | custom-call | flops 1073741824 | bytes 2097152 | tf_op jit(solution)/shard_map/pallas_call | solution.py:69
  108.0 3.9 %shard_map.120 = (f32[512,1024]{1,0:T(8,128)S(1)}, bf16[1024,1024]{1,0:T(8,128)(2,1)S(1)}, bf16[1024,1024]{1,0:T(8,128)(2,1)S(1)}) custom-call(bf16[512,256]{1,0:T(8,128)(2,1)S(1)} %collective-permute-done.39.refs_0_, bf16[512,256]{1,0:T(8,128)(2,1)S(1)} %collective-permute-done.40.refs_1_, ...), custom_call_target="tpu_custom_call", output_to_operand_aliasing={{0}: (5, {})} | custom-call | flops 1073741824 | bytes 2097152 | tf_op jit(solution)/shard_map/pallas_call | solution.py:69
  114.4 2.5 %shard_map.122 = (bf16[512,1024]{1,0:T(8,128)(2,1)S(1)}, bf16[512,1024]{1,0:T(8,128)(2,1)S(1)}) custom-call(bf16[256,256]{1,0:T(8,128)(2,1)S(1)} %collective-permute-done.47.refs_0_, bf16[256,256]{1,0:T(8,128)(2,1)S(1)} %collective-permute-done.48.refs_1_, bf16[1024,256]{1,0:T(8,128)(2,1)S(1)} %get-tuple-element.280.refs_2_, ...), custom_call_target="tpu_custom_call" | custom-call | flops 268435456 | bytes 524288 | tf_op jit(solution)/shard_map/pallas_call | solution.py:69
  118.2 4.5 %shard_map.124 = (f32[512,256]{1,0:T(8,128)S(1)}, f32[512,256]{1,0:T(8,128)S(1)}, bf16[512,256]{1,0:T(8,128)(2,1)S(1)}, bf16[512,256]{1,0:T(8,128)(2,1)S(1)}, bf...) custom-call(bf16[512,1024]{1,0:T(8,128)(2,1)S(1)} %get-tuple-element.285.refs_0_, ...), custom_call_target="tpu_custom_call" | custom-call | flops 2147483648 | bytes 4194304 | tf_op jit(solution)/shard_map/pallas_call | solution.py:69
  125.5 4.6 %shard_map.125 = (f32[512,256]{1,0:T(8,128)S(1)}, f32[512,256]{1,0:T(8,128)S(1)}, bf16[512,256]{1,0:T(8,128)(2,1)S(1)}, bf16[512,256]{1,0:T(8,128)(2,1)S(1)}, bf...) custom-call(bf16[512,1024]{1,0:T(8,128)(2,1)S(1)} %get-tuple-element.285.refs_0_, ...), custom_call_target="tpu_custom_call" | custom-call | flops 2147483648 | bytes 4194304 | tf_op jit(solution)/shard_map/pallas_call | solution.py:69
  133.0 3.9 %shard_map.126 = (f32[512,256]{1,0:T(8,128)S(1)}, f32[512,256]{1,0:T(8,128)S(1)}, bf16[512,256]{1,0:T(8,128)(2,1)S(1)}, bf16[512,256]{1,0:T(8,128)(2,1)S(1)}, bf...) custom-call(bf16[512,1024]{1,0:T(8,128)(2,1)S(1)} %get-tuple-element.285.refs_0_, ...), custom_call_target="tpu_custom_call" | custom-call | flops 2147483648 | bytes 4194304 | tf_op jit(solution)/shard_map/pallas_call | solution.py:69
  136.9 2.2 %collective-permute-done.58 = bf16[512,256]{1,0:T(8,128)(2,1)S(1)} collective-permute-done((bf16[512,256]{1,0:T(8,128)(2,1)S(1)}, bf16[512,256]{1,0:T(8,128)(2,1)S(1)}, u32[]{:S(2)}, u32[]{:S(2)}) %collective-permute-start.58) | collective-permute-done | bytes 262176 | tf_op jit(solution)/shard_map/ppermute | solution.py:275
  140.5 1.6 collective-permute-start.59
  144.0 3.6 %collective-permute-done.61 = bf16[512,256]{1,0:T(8,128)(2,1)S(1)} collective-permute-done((bf16[512,256]{1,0:T(8,128)(2,1)S(1)}, bf16[512,256]{1,0:T(8,128)(2,1)S(1)}, u32[]{:S(2)}, u32[]{:S(2)}) %collective-permute-start.61) | collective-permute-done | bytes 262176 | tf_op jit(solution)/shard_map/ppermute | solution.py:275
  150.3 3.4 %collective-permute-start.33 = (bf16[512,256]{1,0:T(8,128)(2,1)S(1)}, bf16[512,256]{1,0:T(8,128)(2,1)S(1)}, u32[]{:S(2)}, u32[]{:S(2)}) collective-permute-start(bf16[512,256]{1,0:T(8,128)(2,1)S(1)} %get-tuple-element.259), channel_id=1, source_target_pairs={{0,16},{1,17},{2,18},{3,19},{4,20},{5,21},{6,22},{7,23},{8,24},{9,... | collective-permute-start | bytes 786440 | tf_op jit(solution)/shard_map/ppermute | solution.py:451
  157.6 2.3 %collective-permute-done.33 = bf16[512,256]{1,0:T(8,128)(2,1)S(1)} collective-permute-done((bf16[512,256]{1,0:T(8,128)(2,1)S(1)}, bf16[512,256]{1,0:T(8,128)(2,1)S(1)}, u32[]{:S(2)}, u32[]{:S(2)}) %collective-permute-start.33) | collective-permute-done | bytes 262176 | tf_op jit(solution)/shard_map/ppermute | solution.py:451
  160.8 3.8 %collective-permute-done.67 = bf16[512,256]{1,0:T(8,128)(2,1)S(1)} collective-permute-done((bf16[512,256]{1,0:T(8,128)(2,1)S(1)}, bf16[512,256]{1,0:T(8,128)(2,1)S(1)}, u32[]{:S(2)}, u32[]{:S(2)}) %collective-permute-start.67) | collective-permute-done | bytes 262176 | tf_op jit(solution)/shard_map/ppermute | solution.py:452
  (193 shorter events, 67.6 us)
Async XLA Ops:
  1.7 9.3 %collective-permute-start = (bf16[512,256]{1,0:T(8,128)(2,1)S(1)}, bf16[512,256]{1,0:T(8,128)(2,1)S(1)}, u32[]{:S(2)}, u32[]{:S(2)}) collective-permute-start(bf16[512,256]{1,0:T(8,128)(2,1)S(1)} %bitcast.37), channel_id=1, source_target_pairs={{0,4},{1,5},{4,8},{5,9},{8,12},{9,13},{12,14},{13,15},{14,10},{15,... | collective-permute-start | bytes 786440 | tf_op jit(solution)/shard_map/ppermute | solution.py:274
  4.8 7.8 %collective-permute-start.1 = (bf16[512,256]{1,0:T(8,128)(2,1)S(1)}, bf16[512,256]{1,0:T(8,128)(2,1)S(1)}, u32[]{:S(2)}, u32[]{:S(2)}) collective-permute-start(bf16[512,256]{1,0:T(8,128)(2,1)S(1)} %bitcast.38), channel_id=1, source_target_pairs={{4,0},{5,1},{8,4},{9,5},{12,8},{13,9},{14,12},{15,13},{10,14},{11,... | collective-permute-start | bytes 786440 | tf_op jit(solution)/shard_map/ppermute | solution.py:275
  4.8 10.4 %collective-permute-start.4 = (bf16[512,256]{1,0:T(8,128)(2,1)S(1)}, bf16[512,256]{1,0:T(8,128)(2,1)S(1)}, u32[]{:S(2)}, u32[]{:S(2)}) collective-permute-start(bf16[512,256]{1,0:T(8,128)(2,1)S(1)} %bitcast.39), channel_id=1, source_target_pairs={{0,1},{1,0},{4,5},{5,4},{8,9},{9,8},{12,13},{13,12},{14,15},{15,14... | collective-permute-start | bytes 786440 | tf_op jit(solution)/shard_map/ppermute | solution.py:276
  14.7 8.4 %collective-permute-start.7 = (bf16[512,256]{1,0:T(8,128)(2,1)S(1)}, bf16[512,256]{1,0:T(8,128)(2,1)S(1)}, u32[]{:S(2)}, u32[]{:S(2)}) collective-permute-start(bf16[512,256]{1,0:T(8,128)(2,1)S(1)} %collective-permute-done.refs_0_), channel_id=1, source_target_pairs={{0,1},{1,0},{4,5},{5,4},{8,9},{9,8},{12,13},{13,12},{14,15},{15,14... | collective-permute-start | bytes 786440 | tf_op jit(solution)/shard_map/ppermute | solution.py:276
  14.7 8.9 %collective-permute-start.8 = (bf16[512,256]{1,0:T(8,128)(2,1)S(1)}, bf16[512,256]{1,0:T(8,128)(2,1)S(1)}, u32[]{:S(2)}, u32[]{:S(2)}) collective-permute-start(bf16[512,256]{1,0:T(8,128)(2,1)S(1)} %collective-permute-done.1.refs_1_), channel_id=1, source_target_pairs={{0,1},{1,0},{4,5},{5,4},{8,9},{9,8},{12,13},{13,12},{14,15},{15,14... | collective-permute-start | bytes 786440 | tf_op jit(solution)/shard_map/ppermute | solution.py:276
  21.0 7.5 %collective-permute-start.5 = (bf16[512,256]{1,0:T(8,128)(2,1)S(1)}, bf16[512,256]{1,0:T(8,128)(2,1)S(1)}, u32[]{:S(2)}, u32[]{:S(2)}) collective-permute-start(bf16[512,256]{1,0:T(8,128)(2,1)S(1)} %collective-permute-done.2.refs_0_), channel_id=1, source_target_pairs={{0,4},{1,5},{4,8},{5,9},{8,12},{9,13},{12,14},{13,15},{14,10},{15,... | collective-permute-start | bytes 786440 | tf_op jit(solution)/shard_map/ppermute | solution.py:274
  23.1 7.3 %collective-permute-start.11 = (bf16[512,256]{1,0:T(8,128)(2,1)S(1)}, bf16[512,256]{1,0:T(8,128)(2,1)S(1)}, u32[]{:S(2)}, u32[]{:S(2)}) collective-permute-start(bf16[512,256]{1,0:T(8,128)(2,1)S(1)} %collective-permute-done.2.refs_0_), channel_id=1, source_target_pairs={{0,1},{1,0},{4,5},{5,4},{8,9},{9,8},{12,13},{13,12},{14,15},{15,14... | collective-permute-start | bytes 786440 | tf_op jit(solution)/shard_map/ppermute | solution.py:276
  23.1 8.9 %collective-permute-start.12 = (bf16[512,256]{1,0:T(8,128)(2,1)S(1)}, bf16[512,256]{1,0:T(8,128)(2,1)S(1)}, u32[]{:S(2)}, u32[]{:S(2)}) collective-permute-start(bf16[512,256]{1,0:T(8,128)(2,1)S(1)} %collective-permute-done.3.refs_1_), channel_id=1, source_target_pairs={{0,1},{1,0},{4,5},{5,4},{8,9},{9,8},{12,13},{13,12},{14,15},{15,14... | collective-permute-start | bytes 786440 | tf_op jit(solution)/shard_map/ppermute | solution.py:276
  29.3 8.2 %collective-permute-start.15 = (bf16[512,256]{1,0:T(8,128)(2,1)S(1)}, bf16[512,256]{1,0:T(8,128)(2,1)S(1)}, u32[]{:S(2)}, u32[]{:S(2)}) collective-permute-start(bf16[512,256]{1,0:T(8,128)(2,1)S(1)} %collective-permute-done.5.refs_0_), channel_id=1, source_target_pairs={{0,1},{1,0},{4,5},{5,4},{8,9},{9,8},{12,13},{13,12},{14,15},{15,14... | collective-permute-start | bytes 786440 | tf_op jit(solution)/shard_map/ppermute | solution.py:276
  29.3 8.2 %collective-permute-start.16 = (bf16[512,256]{1,0:T(8,128)(2,1)S(1)}, bf16[512,256]{1,0:T(8,128)(2,1)S(1)}, u32[]{:S(2)}, u32[]{:S(2)}) collective-permute-start(bf16[512,256]{1,0:T(8,128)(2,1)S(1)} %collective-permute-done.6.refs_1_), channel_id=1, source_target_pairs={{0,1},{1,0},{4,5},{5,4},{8,9},{9,8},{12,13},{13,12},{14,15},{15,14... | collective-permute-start | bytes 786440 | tf_op jit(solution)/shard_map/ppermute | solution.py:276
  44.9 7.6 %collective-permute-start.21 = (bf16[512,256]{1,0:T(8,128)(2,1)S(1)}, bf16[512,256]{1,0:T(8,128)(2,1)S(1)}, u32[]{:S(2)}, u32[]{:S(2)}) collective-permute-start(bf16[512,256]{1,0:T(8,128)(2,1)S(1)} %get-tuple-element.231), channel_id=1, source_target_pairs={{0,1},{1,0},{4,5},{5,4},{8,9},{9,8},{12,13},{13,12},{14,15},{15,14... | collective-permute-start | bytes 786440 | tf_op jit(solution)/shard_map/ppermute | solution.py:276
  60.3 7.9 %collective-permute-start.27 = (bf16[512,256]{1,0:T(8,128)(2,1)S(1)}, bf16[512,256]{1,0:T(8,128)(2,1)S(1)}, u32[]{:S(2)}, u32[]{:S(2)}) collective-permute-start(bf16[512,256]{1,0:T(8,128)(2,1)S(1)} %add_convert_fusion.8), channel_id=1, source_target_pairs={{4,0},{5,1},{8,4},{9,5},{12,8},{13,9},{14,12},{15,13},{10,14},{11,... | collective-permute-start | bytes 786440 | tf_op jit(solution)/shard_map/ppermute | solution.py:275
  60.9 7.4 %collective-permute-start.25 = (bf16[512,256]{1,0:T(8,128)(2,1)S(1)}, bf16[512,256]{1,0:T(8,128)(2,1)S(1)}, u32[]{:S(2)}, u32[]{:S(2)}) collective-permute-start(bf16[512,256]{1,0:T(8,128)(2,1)S(1)} %add_convert_fusion.9), channel_id=1, source_target_pairs={{0,4},{1,5},{4,8},{5,9},{8,12},{9,13},{12,14},{13,15},{14,10},{15,... | collective-permute-start | bytes 786440 | tf_op jit(solution)/shard_map/ppermute | solution.py:274
  69.1 8.4 %collective-permute-start.32 = (bf16[512,256]{1,0:T(8,128)(2,1)}, bf16[512,256]{1,0:T(8,128)(2,1)S(1)}, u32[]{:S(2)}, u32[]{:S(2)}) collective-permute-start(bf16[512,256]{1,0:T(8,128)(2,1)} %add_convert_fusion.6), channel_id=1, source_target_pairs={{4,0},{5,1},{8,4},{9,5},{12,8},{13,9},{14,12},{15,13},{10,14},{11,... | collective-permute-start | bytes 786440 | tf_op jit(solution)/shard_map/ppermute | solution.py:275
  70.4 8.1 %collective-permute-start.30 = (bf16[512,256]{1,0:T(8,128)(2,1)}, bf16[512,256]{1,0:T(8,128)(2,1)}, u32[]{:S(2)}, u32[]{:S(2)}) collective-permute-start(bf16[512,256]{1,0:T(8,128)(2,1)} %add_convert_fusion.7), channel_id=1, source_target_pairs={{0,4},{1,5},{4,8},{5,9},{8,12},{9,13},{12,14},{13,15},{14,10},{15,... | collective-permute-start | bytes 786440 | tf_op jit(solution)/shard_map/ppermute | solution.py:274
  83.2 8.9 %collective-permute-start.38 = (bf16[512,256]{1,0:T(8,128)(2,1)S(1)}, bf16[512,256]{1,0:T(8,128)(2,1)S(1)}, u32[]{:S(2)}, u32[]{:S(2)}) collective-permute-start(bf16[512,256]{1,0:T(8,128)(2,1)S(1)} %get-tuple-element.260.refs_0_), channel_id=1, source_target_pairs={{0,1},{1,0},{4,5},{5,4},{8,9},{9,8},{12,13},{13,12},{14,15},{15,14... | collective-permute-start | bytes 786440 | tf_op jit(solution)/shard_map/ppermute | solution.py:276
  91.5 8.0 %collective-permute-start.41 = (bf16[512,256]{1,0:T(8,128)(2,1)S(1)}, bf16[512,256]{1,0:T(8,128)(2,1)S(1)}, u32[]{:S(2)}, u32[]{:S(2)}) collective-permute-start(bf16[512,256]{1,0:T(8,128)(2,1)S(1)} %collective-permute-done.34.refs_0_), channel_id=1, source_target_pairs={{0,1},{1,0},{4,5},{5,4},{8,9},{9,8},{12,13},{13,12},{14,15},{15,14... | collective-permute-start | bytes 786440 | tf_op jit(solution)/shard_map/ppermute | solution.py:276
  91.5 8.5 %collective-permute-start.42 = (bf16[512,256]{1,0:T(8,128)(2,1)S(1)}, bf16[512,256]{1,0:T(8,128)(2,1)S(1)}, u32[]{:S(2)}, u32[]{:S(2)}) collective-permute-start(bf16[512,256]{1,0:T(8,128)(2,1)S(1)} %collective-permute-done.35.refs_1_), channel_id=1, source_target_pairs={{0,1},{1,0},{4,5},{5,4},{8,9},{9,8},{12,13},{13,12},{14,15},{15,14... | collective-permute-start | bytes 786440 | tf_op jit(solution)/shard_map/ppermute | solution.py:276
  99.5 7.7 %collective-permute-start.45 = (bf16[512,256]{1,0:T(8,128)(2,1)S(1)}, bf16[512,256]{1,0:T(8,128)(2,1)S(1)}, u32[]{:S(2)}, u32[]{:S(2)}) collective-permute-start(bf16[512,256]{1,0:T(8,128)(2,1)S(1)} %collective-permute-done.36.refs_0_), channel_id=1, source_target_pairs={{0,1},{1,0},{4,5},{5,4},{8,9},{9,8},{12,13},{13,12},{14,15},{15,14... | collective-permute-start | bytes 786440 | tf_op jit(solution)/shard_map/ppermute | solution.py:276
  99.5 8.6 %collective-permute-start.46 = (bf16[512,256]{1,0:T(8,128)(2,1)S(1)}, bf16[512,256]{1,0:T(8,128)(2,1)S(1)}, u32[]{:S(2)}, u32[]{:S(2)}) collective-permute-start(bf16[512,256]{1,0:T(8,128)(2,1)S(1)} %collective-permute-done.37.refs_1_), channel_id=1, source_target_pairs={{0,1},{1,0},{4,5},{5,4},{8,9},{9,8},{12,13},{13,12},{14,15},{15,14... | collective-permute-start | bytes 786440 | tf_op jit(solution)/shard_map/ppermute | solution.py:276
  105.4 7.4 %collective-permute-start.49 = (bf16[512,256]{1,0:T(8,128)(2,1)S(1)}, bf16[512,256]{1,0:T(8,128)(2,1)S(1)}, u32[]{:S(2)}, u32[]{:S(2)}) collective-permute-start(bf16[512,256]{1,0:T(8,128)(2,1)S(1)} %collective-permute-done.39.refs_0_), channel_id=1, source_target_pairs={{0,1},{1,0},{4,5},{5,4},{8,9},{9,8},{12,13},{13,12},{14,15},{15,14... | collective-permute-start | bytes 786440 | tf_op jit(solution)/shard_map/ppermute | solution.py:276
  105.4 7.4 %collective-permute-start.50 = (bf16[512,256]{1,0:T(8,128)(2,1)S(1)}, bf16[512,256]{1,0:T(8,128)(2,1)S(1)}, u32[]{:S(2)}, u32[]{:S(2)}) collective-permute-start(bf16[512,256]{1,0:T(8,128)(2,1)S(1)} %collective-permute-done.40.refs_1_), channel_id=1, source_target_pairs={{0,1},{1,0},{4,5},{5,4},{8,9},{9,8},{12,13},{13,12},{14,15},{15,14... | collective-permute-start | bytes 786440 | tf_op jit(solution)/shard_map/ppermute | solution.py:276
  122.8 7.3 %collective-permute-start.55 = (bf16[512,256]{1,0:T(8,128)(2,1)S(1)}, bf16[512,256]{1,0:T(8,128)(2,1)S(1)}, u32[]{:S(2)}, u32[]{:S(2)}) collective-permute-start(bf16[512,256]{1,0:T(8,128)(2,1)S(1)} %get-tuple-element.309), channel_id=1, source_target_pairs={{0,1},{1,0},{4,5},{5,4},{8,9},{9,8},{12,13},{13,12},{14,15},{15,14... | collective-permute-start | bytes 786440 | tf_op jit(solution)/shard_map/ppermute | solution.py:276
  130.4 8.8 %collective-permute-start.58 = (bf16[512,256]{1,0:T(8,128)(2,1)S(1)}, bf16[512,256]{1,0:T(8,128)(2,1)S(1)}, u32[]{:S(2)}, u32[]{:S(2)}) collective-permute-start(bf16[512,256]{1,0:T(8,128)(2,1)S(1)} %pad_maximum_fusion.3), channel_id=1, source_target_pairs={{4,0},{5,1},{8,4},{9,5},{12,8},{13,9},{14,12},{15,13},{10,14},{11,... | collective-permute-start | bytes 786440 | tf_op jit(solution)/shard_map/ppermute | solution.py:275
  131.3 8.5 %collective-permute-start.56 = (bf16[512,256]{1,0:T(8,128)(2,1)S(1)}, bf16[512,256]{1,0:T(8,128)(2,1)S(1)}, u32[]{:S(2)}, u32[]{:S(2)}) collective-permute-start(bf16[512,256]{1,0:T(8,128)(2,1)S(1)} %pad_maximum_fusion.2), channel_id=1, source_target_pairs={{0,4},{1,5},{4,8},{5,9},{8,12},{9,13},{12,14},{13,15},{14,10},{15,... | collective-permute-start | bytes 786440 | tf_op jit(solution)/shard_map/ppermute | solution.py:274
  132.5 7.3 %collective-permute-start.60 = (bf16[512,256]{1,0:T(8,128)(2,1)S(1)}, bf16[512,256]{1,0:T(8,128)(2,1)S(1)}, u32[]{:S(2)}, u32[]{:S(2)}) collective-permute-start(bf16[512,256]{1,0:T(8,128)(2,1)S(1)} %get-tuple-element.323), channel_id=1, source_target_pairs={{0,1},{1,0},{4,5},{5,4},{8,9},{9,8},{12,13},{13,12},{14,15},{15,14... | collective-permute-start | bytes 786440 | tf_op jit(solution)/shard_map/ppermute | solution.py:276
  132.5 7.9 %collective-permute-start.54 = (bf16[512,256]{1,0:T(8,128)(2,1)S(1)}, bf16[512,256]{1,0:T(8,128)(2,1)S(1)}, u32[]{:S(2)}, u32[]{:S(2)}) collective-permute-start(bf16[512,256]{1,0:T(8,128)(2,1)S(1)} %get-tuple-element.307), channel_id=1, source_target_pairs={{0,1},{1,0},{4,5},{5,4},{8,9},{9,8},{12,13},{13,12},{14,15},{15,14... | collective-permute-start | bytes 786440 | tf_op jit(solution)/shard_map/ppermute | solution.py:276
  139.9 7.7 %collective-permute-start.61 = (bf16[512,256]{1,0:T(8,128)(2,1)S(1)}, bf16[512,256]{1,0:T(8,128)(2,1)S(1)}, u32[]{:S(2)}, u32[]{:S(2)}) collective-permute-start(bf16[512,256]{1,0:T(8,128)(2,1)S(1)} %add_convert_fusion.3), channel_id=1, source_target_pairs={{4,0},{5,1},{8,4},{9,5},{12,8},{13,9},{14,12},{15,13},{10,14},{11,... | collective-permute-start | bytes 786440 | tf_op jit(solution)/shard_map/ppermute | solution.py:275
  140.5 7.5 %collective-permute-start.59 = (bf16[512,256]{1,0:T(8,128)(2,1)S(1)}, bf16[512,256]{1,0:T(8,128)(2,1)S(1)}, u32[]{:S(2)}, u32[]{:S(2)}) collective-permute-start(bf16[512,256]{1,0:T(8,128)(2,1)S(1)} %add_convert_fusion.4), channel_id=1, source_target_pairs={{0,4},{1,5},{4,8},{5,9},{8,12},{9,13},{12,14},{13,15},{14,10},{15,... | collective-permute-start | bytes 786440 | tf_op jit(solution)/shard_map/ppermute | solution.py:274
  142.2 7.5 %collective-permute-start.65 = (bf16[512,256]{1,0:T(8,128)(2,1)S(1)}, bf16[512,256]{1,0:T(8,128)(2,1)S(1)}, u32[]{:S(2)}, u32[]{:S(2)}) collective-permute-start(bf16[512,256]{1,0:T(8,128)(2,1)S(1)} %get-tuple-element.335), channel_id=1, source_target_pairs={{0,1},{1,0},{4,5},{5,4},{8,9},{9,8},{12,13},{13,12},{14,15},{15,14... | collective-permute-start | bytes 786440 | tf_op jit(solution)/shard_map/ppermute | solution.py:276
  150.3 9.6 %collective-permute-start.33 = (bf16[512,256]{1,0:T(8,128)(2,1)S(1)}, bf16[512,256]{1,0:T(8,128)(2,1)S(1)}, u32[]{:S(2)}, u32[]{:S(2)}) collective-permute-start(bf16[512,256]{1,0:T(8,128)(2,1)S(1)} %get-tuple-element.259), channel_id=1, source_target_pairs={{0,16},{1,17},{2,18},{3,19},{4,20},{5,21},{6,22},{7,23},{8,24},{9,... | collective-permute-start | bytes 786440 | tf_op jit(solution)/shard_map/ppermute | solution.py:451
  156.3 8.3 %collective-permute-start.67 = (bf16[512,256]{1,0:T(8,128)(2,1)S(1)}, bf16[512,256]{1,0:T(8,128)(2,1)S(1)}, u32[]{:S(2)}, u32[]{:S(2)}) collective-permute-start(bf16[512,256]{1,0:T(8,128)(2,1)S(1)} %add_convert_fusion), channel_id=1, source_target_pairs={{16,0},{17,1},{18,2},{19,3},{20,4},{21,5},{22,6},{23,7},{24,8},{25... | collective-permute-start | bytes 786440 | tf_op jit(solution)/shard_map/ppermute | solution.py:452
  (46 other events, 244.0 us)
